TPU v7x, 256 devices: a whole 4x4x8 slice. The times are simulated.
256 devices in a mesh: ctx: 32 (over x, y, core), grp: 8 (over z).
Axes of the slice: x: 4, y: 4, z: 8, core: 2. Of those that a mesh axis runs over, the one named last changes fastest.
Arguments:
- window_states: bfloat16 [8, 64, 8192], P('grp'), may hold values from -6 to 6
- query_weight: bfloat16 [8192, 8192], P('grp', 'ctx'), may hold values from -0.0625 to 0.0625
- cache_keys: bfloat16 [8, 16384, 1024], P('grp', 'ctx'), may hold values from -65 to 65
- cache_values: bfloat16 [8, 16384, 1024], P('grp', 'ctx'), may hold values from -6 to 6
- kept_blocks: int32 [8, 8, 32], P('grp', None, 'ctx'), may hold values from 0 to 127, as said below
- retained_block_count: int32 [8, 8, 32], P('grp', None, 'ctx'), may hold values from 0 to 1, as said below
- decode_queries: bfloat16 [8, 4, 32, 8192], P('grp', None, 'ctx'), may hold values from -9 to 9
- tail_keys: bfloat16 [8, 32, 64, 1024], P('grp', 'ctx'), may hold values from -6 to 6
- tail_values: bfloat16 [8, 32, 64, 1024], P('grp', 'ctx'), may hold values from -6 to 6
- row_lengths: int32 [8, 32], P('grp', 'ctx'), may hold values from 2 to 61, as said below
Outputs:
- pooled_votes: float32 [8, 8, 16384], P('grp', None, 'ctx')
- decode_out: bfloat16 [8, 4, 32, 8192], P('grp', None, 'ctx')
Inputs may be any that keep to these rules, and one draw needn't show every extreme that they name: `kept_blocks`: for key head k, entry c names one block held by ctx index c, that is one of the blocks c * 4 to c * 4 + 3; it is kept only if retained_block_count[g, k, c] is 1. `retained_block_count`: in every request some device holds 1 kept blocks for every key head. `row_lengths`: 61 is reached in every request.
All inputs are finite; a program needn't handle non-finite values.
Results may differ from a plain program's by a relative error of at most 0.0019.
Values may be sent and summed in bfloat16 or wider, within the bound.
A program may use at most 128 MiB of HBM per device.

v0:
```python
import math

import jax
import jax.numpy as jnp
from jax import lax
from jax.sharding import PartitionSpec as P

KEY_HEADS = 8
HEAD_DIMENSION = 128
BLOCK_POSITIONS = 128
POOL = 7


def combined_all(part, axis, combine):
    gathered = jax.tree.map(lambda a: lax.all_gather(a, axis), part)

    def take(source):
        return jax.tree.map(lambda a: lax.dynamic_index_in_dim(a, source, 0, False), gathered)

    return lax.fori_loop(
        1, lax.axis_size(axis), lambda source, state: combine(state, take(source)), take(0)
    )


def padded_2(cells, sides, width):
    for axis, dim in sides:
        count = lax.axis_size(axis)
        ends = count - 1
        head = lax.slice_in_dim(cells, 0, width, axis=dim)
        tail = lax.slice_in_dim(cells, cells.shape[dim] - width, cells.shape[dim], axis=dim)
        cells = jnp.concatenate(
            [
                lax.ppermute(tail, axis, [(i, (i + 1) % count) for i in range(ends)]),
                cells,
                lax.ppermute(head, axis, [((i + 1) % count, i) for i in range(ends)]),
            ],
            axis=dim,
        )
    return cells


def rotary_table(positions, head_size):
    exponent = jnp.arange(0, head_size, 2).astype(jnp.float32) / head_size
    inverse = jnp.power(jnp.float32(500000.0), -exponent)
    wavelength = 2.0 * math.pi / inverse
    smooth = (8192.0 / wavelength - 1.0) / 3.0
    blended = (1.0 - smooth) * inverse / 8.0 + smooth * inverse
    adjusted = jnp.where(
        wavelength > 8192.0, inverse / 8.0, jnp.where(wavelength < 2048.0, inverse, blended)
    )
    angles = positions[:, None] * adjusted[None, :]
    return (jnp.cos(angles), jnp.sin(angles))


def rotate(vectors, cosine_table, sine_table):
    half_size = vectors.shape[-1] // 2
    leading = vectors[..., :half_size]
    trailing = vectors[..., half_size:]
    cosine_part = cosine_table[:, None, :]
    sine_part = sine_table[:, None, :]
    return jnp.concatenate(
        [
            leading * cosine_part - trailing * sine_part,
            trailing * cosine_part + leading * sine_part,
        ],
        axis=-1,
    )


def merge_stats(earlier, later):
    highest = jnp.maximum(earlier[0], later[0])
    return (
        highest,
        earlier[1] * jnp.exp(earlier[0] - highest) + later[1] * jnp.exp(later[0] - highest),
    )


def on_device(
    window_states,
    query_weight,
    cache_keys,
    cache_values,
    kept_blocks,
    retained_block_count,
    decode_queries,
    tail_keys,
    tail_values,
    row_lengths,
):
    ctx_count = lax.axis_size("ctx")
    ctx_index = lax.axis_index("ctx")
    states = window_states[0]
    win_rows = states.shape[0]
    local_cols = query_weight.shape[1]
    local_heads = local_cols // HEAD_DIMENSION
    projected = jnp.dot(
        states,
        lax.all_gather(query_weight, "grp", axis=0, tiled=True),
        preferred_element_type=jnp.float32,
    )
    local_keys = cache_keys[0]
    ctx_local = local_keys.shape[0]
    total_ctx = ctx_local * ctx_count
    start_pos = total_ctx - win_rows
    positions = (jnp.arange(win_rows) + start_pos).astype(jnp.float32)
    cosine_table, sine_table = rotary_table(positions, HEAD_DIMENSION)
    turned = rotate(
        projected.reshape(win_rows, local_heads, HEAD_DIMENSION), cosine_table, sine_table
    )
    window_local = turned.reshape(win_rows, local_cols).astype(jnp.bfloat16)
    window_all, decode_all = (
        lax.all_gather(window_local, "ctx", axis=1, tiled=True),
        lax.all_gather(decode_queries[0], "ctx", axis=1, tiled=True),
    )
    head_total = window_all.shape[1] // HEAD_DIMENSION
    group_size = head_total // KEY_HEADS
    key_scale = 1.0 / math.sqrt(HEAD_DIMENSION)
    key_positions = ctx_index * ctx_local + jnp.arange(ctx_local)
    allowed = key_positions[None, :] <= (start_pos + jnp.arange(win_rows))[:, None]
    exp_list = []
    max_list = []
    sum_list = []
    for head_index in range(KEY_HEADS):
        head_queries = window_all[
            :,
            head_index
            * group_size
            * HEAD_DIMENSION : (head_index + 1)
            * group_size
            * HEAD_DIMENSION,
        ].reshape(win_rows, group_size, HEAD_DIMENSION)
        key_head_rows = local_keys[
            :, head_index * HEAD_DIMENSION : (head_index + 1) * HEAD_DIMENSION
        ]
        scores = (
            jnp.einsum(
                "wgd,td->gwt", head_queries, key_head_rows, preferred_element_type=jnp.float32
            )
            * key_scale
        )
        scores = jnp.where(allowed[None], scores, -1e30)
        head_max = jnp.max(scores, axis=-1)
        exponent_values = jnp.where(allowed[None], jnp.exp(scores - head_max[..., None]), 0.0)
        exp_list.append(exponent_values)
        max_list.append(head_max)
        sum_list.append(jnp.sum(exponent_values, axis=-1))
    exponentials = jnp.stack(exp_list)
    local_max = jnp.stack(max_list).reshape(head_total, win_rows)
    local_sum = jnp.stack(sum_list).reshape(head_total, win_rows)
    merged_max, merged_sum = combined_all((local_max, local_sum), "ctx", merge_stats)
    coefficient = (jnp.exp(local_max - merged_max) / merged_sum).reshape(
        KEY_HEADS, group_size, win_rows
    )
    vote_sums = jnp.sum(coefficient[..., None] * exponentials, axis=(1, 2)) * (
        total_ctx / (win_rows * group_size)
    )
    half_width = (POOL - 1) // 2
    padded = padded_2(vote_sums, (("ctx", 1),), half_width)
    pooled = padded[:, 0:ctx_local]
    for shift_index in range(1, POOL):
        pooled = pooled + padded[:, shift_index : shift_index + ctx_local]
    pooled_votes = (pooled / POOL)[None]
    step_count = decode_all.shape[0]
    rows_all = decode_all.shape[1]
    rows_local = decode_queries.shape[2]
    total_rows = step_count * rows_all
    block_total = ctx_local // BLOCK_POSITIONS
    keys_local = local_keys.reshape(block_total, BLOCK_POSITIONS, KEY_HEADS, HEAD_DIMENSION)
    values_local = cache_values[0].reshape(block_total, BLOCK_POSITIONS, KEY_HEADS, HEAD_DIMENSION)
    local_blocks = kept_blocks[0] - ctx_index * block_total
    local_counts = retained_block_count[0, :, 0]
    rounds = jnp.max(local_counts)
    grouped = decode_all.reshape(total_rows, KEY_HEADS, group_size, HEAD_DIMENSION)
    head_range = jnp.arange(KEY_HEADS)

    def visit_slot(position, state_now):
        run_max, run_sum, run_acc = state_now
        chosen = lax.dynamic_index_in_dim(local_blocks, position, 1, keepdims=False)
        key_block = keys_local[chosen, :, head_range, :]
        value_block = values_local[chosen, :, head_range, :]
        is_live = (position < local_counts)[None, :, None, None]
        scores = (
            jnp.einsum("rhgd,htd->rhgt", grouped, key_block, preferred_element_type=jnp.float32)
            * key_scale
        )
        scores = jnp.where(is_live, scores, -1e30)
        new_max = jnp.maximum(run_max, jnp.max(scores, axis=-1))
        rescale = jnp.exp(run_max - new_max)
        weights = jnp.where(is_live, jnp.exp(scores - new_max[..., None]), 0.0)
        run_sum = run_sum * rescale + jnp.sum(weights, axis=-1)
        run_acc = run_acc * rescale[..., None] + jnp.einsum(
            "rhgt,htd->rhgd",
            weights,
            value_block.astype(jnp.float32),
            precision=lax.Precision.HIGHEST,
        )
        return (new_max, run_sum, run_acc)

    initial = (
        jnp.full((total_rows, KEY_HEADS, group_size), -1e30, jnp.float32),
        jnp.zeros((total_rows, KEY_HEADS, group_size), jnp.float32),
        jnp.zeros((total_rows, KEY_HEADS, group_size, HEAD_DIMENSION), jnp.float32),
    )
    run_max, run_sum, run_acc = lax.fori_loop(0, rounds, visit_slot, initial)
    cache_max = run_max.reshape(step_count, rows_all, head_total)
    cache_sum = run_sum.reshape(step_count, rows_all, head_total)
    cache_acc = run_acc.reshape(step_count, rows_all, head_total * HEAD_DIMENSION)
    tail_len = tail_keys.shape[2]
    own_queries = decode_queries[0].reshape(
        step_count, rows_local, KEY_HEADS, group_size, HEAD_DIMENSION
    )
    tail_key_rows = tail_keys[0].reshape(rows_local, tail_len, KEY_HEADS, HEAD_DIMENSION)
    tail_value_rows = tail_values[0].reshape(rows_local, tail_len, KEY_HEADS, HEAD_DIMENSION)
    visible = (
        jnp.arange(tail_len)[None, None, :]
        < row_lengths[0][None, :, None] + jnp.arange(step_count)[:, None, None]
    )
    visible = visible[:, :, None, None, :]
    tail_scores = (
        jnp.einsum(
            "srhgd,rjhd->srhgj", own_queries, tail_key_rows, preferred_element_type=jnp.float32
        )
        * key_scale
    )
    tail_scores = jnp.where(visible, tail_scores, -1e30)
    tail_max = jnp.max(tail_scores, axis=-1)
    tail_weights = jnp.where(visible, jnp.exp(tail_scores - tail_max[..., None]), 0.0)
    tail_sum = jnp.sum(tail_weights, axis=-1).reshape(step_count, rows_local, head_total)
    tail_acc = jnp.einsum(
        "srhgj,rjhd->srhgd",
        tail_weights,
        tail_value_rows.astype(jnp.float32),
        precision=lax.Precision.HIGHEST,
    )
    tail_acc = tail_acc.reshape(step_count, rows_local, head_total, HEAD_DIMENSION)
    tail_max = tail_max.reshape(step_count, rows_local, head_total)
    received_acc, received_max, received_sum = (
        lax.all_to_all(cache_acc[None], "ctx", split_axis=2, concat_axis=0, tiled=True),
        lax.all_to_all(cache_max[None], "ctx", split_axis=2, concat_axis=0, tiled=True),
        lax.all_to_all(cache_sum[None], "ctx", split_axis=2, concat_axis=0, tiled=True),
    )
    peak_value = jnp.maximum(jnp.max(received_max, axis=0), tail_max)
    factors = jnp.exp(received_max - peak_value[None])
    tail_factor = jnp.exp(tail_max - peak_value)
    spread_acc = received_acc.reshape(
        received_acc.shape[0], step_count, rows_local, head_total, HEAD_DIMENSION
    )
    numerator = jnp.sum(spread_acc * factors[..., None], axis=0) + tail_acc * tail_factor[..., None]
    denominator = jnp.sum(received_sum * factors, axis=0) + tail_sum * tail_factor
    decode_out = (
        (numerator / denominator[..., None])
        .reshape(step_count, rows_local, head_total * HEAD_DIMENSION)
        .astype(jnp.bfloat16)[None]
    )
    return (pooled_votes, decode_out)


def solution(mesh):
    placed = (
        P("grp", None, None),
        P("grp", "ctx"),
        P("grp", "ctx", None),
        P("grp", "ctx", None),
        P("grp", None, "ctx"),
        P("grp", None, "ctx"),
        P("grp", None, "ctx", None),
        P("grp", "ctx", None, None),
        P("grp", "ctx", None, None),
        P("grp", "ctx"),
    )
    return jax.shard_map(
        on_device,
        mesh=mesh,
        in_specs=placed,
        out_specs=(P("grp", None, "ctx"), P("grp", None, "ctx", None)),
        check_vma=False,
    )
```

profile of v0, /device:TPU:1, one launch (start us, length us, event | category | flops | bytes accessed | tf_op | source)
XLA Modules:
  0.0 338.1 jit_solution(13341545864074250296)
XLA Ops:
  13.5 50.1 %all-gather.9.cloned.1.call-done = bf16[1,4,32,8192]{3,1,0,2:T(4,128)(2,1)} async-done(((bf16[1,4,1,8192]{3,1,0,2:T(4,128)(2,1)}), bf16[1,4,32,8192]{3,1,0,2:T(4,128)(2,1)}) %all-gather.9.cloned.1.call-update) | async-done | bytes 2097168 | tf_op jit(solution)/shard_map/all_gather | solution.py:113
  63.7 2.7 copy.200
  68.4 2.5 broadcast_in_dim.186
  70.9 12.0 %while.34 = (s32[]{:T(128)}, f32[128,8,8]{0,2,1:T(8,128)S(1)}, f32[128,8,8]{0,2,1:T(8,128)S(1)}, f32[128,8,8,128]{3,0,2,1:T(8,128)}, s32[]{:T(128)}, /*index=5*/...) while((s32[]{:T(128)}, f32[128,8,8]{0,2,1:T(8,128)S(1)}, ...), condition=%wide.region_23.24_spmd, body=%wide.region_20.23_spmd.sunk | while | flops 1893744640 | bytes 57671904 | solution.py:204
  71.6 1.9 bitcast_reduce_fusion.3
  74.8 5.4 %bitcast_add_fusion.2 = f32[128,8,8,128]{3,0,2,1:T(8,128)S(1)} fusion(f32[128,8,8,128]{3,0,2,1:T(8,128)S(1)} %copy-done.1, f32[128,8,8]{0,2,1:T(8,128)S(1)} %get-tuple-element.508, f32[8,128,128,8]{2,1,3,0:T(8,128)S(1)} %get-tuple-element.506, f32[128,8,8]{0,2,1:T(8,128)S(1)} %max.37, pred[8]{0:T(512)(128)(4,1)S(1)} %broadcast_compare_fusion.3, ...), kind=kOutput, calls=%fused_computation.7.clone.1 | convolution fusion | flops 1616904192 | bytes 12910600 | tf_op jit(solution)/shard_map/while/body/rhgt,htd->rhgd/dot_general | solution.py:191
  80.3 2.0 copy-done.2
  83.9 5.1 %all-to-all-start.1 = ((f32[32,1,256]{2,1,0:T(1,128)}), f32[32,1,256]{2,1,0:T(1,128)S(1)}, u32[]{:S(2)}, u32[]{:S(2)}) async-start(f32[32,1,256]{2,1,0:T(1,128)} %reshape.469), calls=%async_computation.1 | async-start | bytes 65536 | tf_op jit(solution)/shard_map/all_to_all | solution.py:239
  89.9 6.3 %all-to-all-done.1 = f32[32,1,256]{2,1,0:T(1,128)S(1)} async-done(((f32[32,1,256]{2,1,0:T(1,128)}), f32[32,1,256]{2,1,0:T(1,128)S(1)}, u32[]{:S(2)}, u32[]{:S(2)}) %all-to-all-start.1) | async-done | bytes 32800 | tf_op jit(solution)/shard_map/all_to_all | solution.py:239
  96.3 3.9 %all-to-all-start.2 = ((f32[32,1,256]{2,1,0:T(1,128)}), f32[32,1,256]{2,1,0:T(1,128)S(1)}, u32[]{:S(2)}, u32[]{:S(2)}) async-start(f32[32,1,256]{2,1,0:T(1,128)} %reshape.471), calls=%async_computation.2 | async-start | bytes 65536 | tf_op jit(solution)/shard_map/all_to_all | solution.py:240
  100.2 6.6 %copy.203 = f32[128,8,8,128]{3,2,1,0:T(8,128)} copy(f32[128,8,8,128]{3,0,2,1:T(8,128)} %get-tuple-element.265) | data formatting | bytes 8388608 | tf_op jit(solution)/shard_map/while | solution.py:204
  106.8 5.0 %broadcast_in_dim_reshape.10 = f32[1,4,32,8192]{3,2,1,0:T(8,128)} reshape(f32[128,8,8,128]{3,2,1,0:T(8,128)} %copy.203) | data formatting | bytes 8388608 | tf_op jit(solution)/shard_map/broadcast_in_dim;reshape | solution.py:238
  111.8 6.9 %copy.204 = f32[1,4,32,8192]{3,1,0,2:T(4,128)} copy(f32[1,4,32,8192]{3,2,1,0:T(8,128)} %broadcast_in_dim_reshape.10) | data formatting | bytes 8388608 | tf_op jit(solution)/shard_map/broadcast_in_dim;reshape | solution.py:238
  118.7 7.7 %all-to-all-start = ((f32[1,4,32,8192]{3,1,0,2:T(4,128)}), f32[1,4,32,8192]{3,1,0,2:T(4,128)}, u32[]{:S(2)}, u32[]{:S(2)}) async-start(f32[1,4,32,8192]{3,1,0,2:T(4,128)} %copy.204), calls=%async_computation | async-start | bytes 8388608 | tf_op jit(solution)/shard_map/all_to_all | solution.py:238
  131.1 2.6 mul.307
  133.6 5.5 %mul.308 = f32[32,1,4,1,8192]{4,2,0,3,1:T(4,128)} reshape(f32[32,4,64,128]{3,2,1,0:T(8,128)} %mul.307) | data formatting | bytes 8388608 | tf_op jit(solution)/shard_map/mul | solution.py:248
  139.2 6.4 %copy.179 = bf16[256,8192]{1,0:T(8,128)(2,1)} copy(bf16[256,8192]{0,1:T(8,128)(2,1)} %bitcast.316) | data formatting | bytes 8388608 | tf_op jit(solution)/shard_map/dot_general | solution.py:96
  145.6 3.6 %fusion.40 = f32[64,2,128]{2,0,1:T(8,128)S(1)} fusion(bf16[2,128,8192]{2,1,0:T(8,128)(2,1)} %bitcast.313, bf16[1,64,8192]{2,1,0:T(8,128)(2,1)S(1)} %copy-done), kind=kOutput, calls=%fused_computation.69 | convolution fusion | flops 268435456 | bytes 5308416 | tf_op jit(solution)/shard_map/dot_general | solution.py:96
  150.0 29.2 %all-to-all-done = f32[1,4,32,8192]{3,1,0,2:T(4,128)} async-done(((f32[1,4,32,8192]{3,1,0,2:T(4,128)}), f32[1,4,32,8192]{3,1,0,2:T(4,128)}, u32[]{:S(2)}, u32[]{:S(2)}) %all-to-all-start) | async-done | bytes 4194336 | tf_op jit(solution)/shard_map/all_to_all | solution.py:238
  179.2 5.2 %fusion.21 = f32[4,8192]{1,0:T(4,128)S(1)} fusion(f32[32,1,4,1,8192]{4,2,0,3,1:T(4,128)} %mul.308, f32[1,4,32,8192]{3,1,0,2:T(4,128)} %all-to-all-done), kind=kLoop, calls=%fused_computation.32 | loop fusion | flops 2064384 | bytes 8519680 | tf_op jit(solution)/shard_map/reduce_sum | solution.py:248
  185.5 19.0 %all-gather.7.cloned.1.call-done = bf16[64,8192]{1,0:T(8,128)(2,1)} async-done(((bf16[64,256]{1,0:T(8,128)(2,1)}), bf16[64,8192]{1,0:T(8,128)(2,1)}) %all-gather.7.cloned.1.call-update) | async-done | bytes 1048592 | tf_op jit(solution)/shard_map/all_gather | solution.py:112
  212.9 1.5 fusion.90
  214.5 1.5 fusion.91
  216.1 1.5 fusion.92
  219.0 3.6 %fusion.49 = (f32[8,64]{0,1:T(8,128)S(1)}, f32[8,64]{0,1:T(8,128)}, f32[8,64]{0,1:T(8,128)}, f32[8,64]{0,1:T(8,128)}, f32[8,64]{0,1:T(8,128)}, /*index=5*/f32[8,...) fusion(f32[8,64,512]{2,0,1:T(8,128)S(1)} %get-tuple-element.407, f32[8,64]{0,1:T(8,128)S(1)} %get-tuple-element.406, ...), kind=kLoop, calls=%fused_computation.86 | loop fusion | flops 6287360 | bytes 8454144 | tf_op jit(solution)/shard_map/reduce_sum | solution.py:146
  232.9 24.6 %all_gather.18 = f32[32,64,64]{2,1,0:T(8,128)S(1)} all-gather(f32[1,64,64]{2,1,0:T(8,128)} %bitcast.365), channel_id=1, replica_groups=mesh['ctx'=32,'grp'=8] {'ctx'}, dimensions={0}, use_global_device_ids=true | all-gather | bytes 540672 | tf_op jit(solution)/shard_map/all_gather | solution.py:15
  259.1 22.8 %all_gather.17 = f32[32,64,64]{2,1,0:T(8,128)S(1)} all-gather(f32[1,64,64]{2,1,0:T(8,128)S(1)} %bitcast.350), channel_id=1, replica_groups=mesh['ctx'=32,'grp'=8] {'ctx'}, dimensions={0}, use_global_device_ids=true | all-gather | bytes 540672 | tf_op jit(solution)/shard_map/all_gather | solution.py:15
  282.8 25.9 %while.33 = (s32[]{:T(128)}, f32[64,64]{1,0:T(8,128)S(1)}, f32[64,64]{1,0:T(8,128)S(1)}, f32[32,64,64]{2,1,0:T(8,128)}, f32[32,64,64]{2,1,0:T(8,128)}, /*index=5*/s32[]{:T(128)}, s32[]{:T(128)}, s32[]{:T(128)}) while((s32[]{:T(128)}, f32[64,64]{1,0:T(8,128)S(1)}, f32[64,64]{1,0:T(8,128)S(1)}, f32[32,64,64]{2,1,0:T(8,128)}, ...), condition=%wide.region_17.18_spmd, body=%wide.region_16.17_spmd.sunk | while | flops 24581 | bytes 98435 | solution.py:20
  319.2 3.8 %multiply_reduce_fusion = f32[8,512]{1,0:T(8,128)S(1)} fusion(f32[8,8,64,512]{3,1,2,0:T(8,128)} %bitcast_dynamic-update-slice_fusion, f32[8,8,64]{1,2,0:T(8,128)S(1)} %copy.197), kind=kLoop, calls=%fused_computation.30 | loop fusion | flops 4190208 | bytes 8421376 | tf_op jit(solution)/shard_map/reduce_sum | solution.py:154
  323.1 2.8 collective-permute-start
  325.9 1.9 collective-permute-start.1
  327.9 3.0 collective-permute-done.1
  (215 shorter events, 76.4 us)
Async XLA Ops:
  7.2 138.4 %copy-start = (bf16[1,64,8192]{2,1,0:T(8,128)(2,1)S(1)}, bf16[1,64,8192]{2,1,0:T(8,128)(2,1)}, u32[]{:S(2)}) copy-start(bf16[1,64,8192]{2,1,0:T(8,128)(2,1)} %param.14) | copy-start | bytes 3145732
  7.2 3.3 copy-start.15
  7.2 56.5 %all-gather.9.cloned.1.call-start = ((), (), s32[]{:S(2)}) async-start(), calls=%async_computation.5 | async-start | bytes 2162688 | tf_op jit(solution)/shard_map/all_gather | solution.py:113
  7.9 131.3 %all-gather.5.cloned.1.call-start = ((), (), s32[]{:S(2)}) async-start(), calls=%async_computation.3 | async-start | bytes 4718592 | tf_op jit(solution)/shard_map/all_gather | solution.py:98
  10.2 2.7 copy-start.28
  71.6 3.3 copy-start.1
  83.9 12.4 %all-to-all-start.1 = ((f32[32,1,256]{2,1,0:T(1,128)}), f32[32,1,256]{2,1,0:T(1,128)S(1)}, u32[]{:S(2)}, u32[]{:S(2)}) async-start(f32[32,1,256]{2,1,0:T(1,128)} %reshape.469), calls=%async_computation.1 | async-start | bytes 65536 | tf_op jit(solution)/shard_map/all_to_all | solution.py:239
  96.3 22.4 %all-to-all-start.2 = ((f32[32,1,256]{2,1,0:T(1,128)}), f32[32,1,256]{2,1,0:T(1,128)S(1)}, u32[]{:S(2)}, u32[]{:S(2)}) async-start(f32[32,1,256]{2,1,0:T(1,128)} %reshape.471), calls=%async_computation.2 | async-start | bytes 65536 | tf_op jit(solution)/shard_map/all_to_all | solution.py:240
  118.7 8.6 %copy-start.24 = (bf16[1,1,64,1024]{3,2,1,0:T(8,128)(2,1)S(1)}, bf16[1,1,64,1024]{3,2,1,0:T(8,128)(2,1)}, u32[]{:S(2)}) copy-start(bf16[1,1,64,1024]{3,2,1,0:T(8,128)(2,1)} %param.21) | copy-start | bytes 393220
  118.7 8.7 %copy-start.26 = (bf16[1,4,1,8192]{3,1,2,0:T(4,128)(2,1)S(1)}, bf16[1,4,1,8192]{3,1,2,0:T(4,128)(2,1)}, u32[]{:S(2)}) copy-start(bf16[1,4,1,8192]{3,1,2,0:T(4,128)(2,1)} %param.20) | copy-start | bytes 196612
  118.7 9.4 %copy-start.25 = (bf16[1,1,64,1024]{3,2,1,0:T(8,128)(2,1)S(1)}, bf16[1,1,64,1024]{3,2,1,0:T(8,128)(2,1)}, u32[]{:S(2)}) copy-start(bf16[1,1,64,1024]{3,2,1,0:T(8,128)(2,1)} %param.22) | copy-start | bytes 393220
  118.7 60.5 %all-to-all-start = ((f32[1,4,32,8192]{3,1,0,2:T(4,128)}), f32[1,4,32,8192]{3,1,0,2:T(4,128)}, u32[]{:S(2)}, u32[]{:S(2)}) async-start(f32[1,4,32,8192]{3,1,0,2:T(4,128)} %copy.204), calls=%async_computation | async-start | bytes 8388608 | tf_op jit(solution)/shard_map/all_to_all | solution.py:238
  126.4 78.1 %all-gather.7.cloned.1.call-start = ((), (), s32[]{:S(2)}) async-start(), calls=%async_computation.4 | async-start | bytes 1081344 | tf_op jit(solution)/shard_map/all_gather | solution.py:112
  211.3 7.6 %copy-start.3 = (f32[8,64,512]{2,0,1:T(8,128)}, f32[8,64,512]{2,0,1:T(8,128)S(1)}, u32[]{:S(2)}) copy-start(f32[8,64,512]{2,0,1:T(8,128)S(1)} %get-tuple-element.399) | copy-start | bytes 3145732
  212.9 9.6 %copy-start.5 = (f32[8,64,512]{2,0,1:T(8,128)}, f32[8,64,512]{2,0,1:T(8,128)S(1)}, u32[]{:S(2)}) copy-start(f32[8,64,512]{2,0,1:T(8,128)S(1)} %get-tuple-element.401) | copy-start | bytes 3145732
  212.9 45.8 %copy-start.16 = (f32[8,64]{0,1:T(8,128)}, f32[8,64]{0,1:T(8,128)S(1)}, u32[]{:S(2)}) copy-start(f32[8,64]{0,1:T(8,128)S(1)} %get-tuple-element.400) | copy-start | bytes 6148
  214.5 8.1 %copy-start.7 = (f32[8,64,512]{2,0,1:T(8,128)}, f32[8,64,512]{2,0,1:T(8,128)S(1)}, u32[]{:S(2)}) copy-start(f32[8,64,512]{2,0,1:T(8,128)S(1)} %get-tuple-element.403) | copy-start | bytes 3145732
  214.5 44.3 %copy-start.18 = (f32[8,64]{0,1:T(8,128)}, f32[8,64]{0,1:T(8,128)S(1)}, u32[]{:S(2)}) copy-start(f32[8,64]{0,1:T(8,128)S(1)} %get-tuple-element.402) | copy-start | bytes 6148
  216.0 6.5 %copy-start.9 = (f32[8,64,512]{2,0,1:T(8,128)}, f32[8,64,512]{2,0,1:T(8,128)S(1)}, u32[]{:S(2)}) copy-start(f32[8,64,512]{2,0,1:T(8,128)S(1)} %get-tuple-element.405) | copy-start | bytes 3145732
  216.1 42.8 %copy-start.20 = (f32[8,64]{0,1:T(8,128)}, f32[8,64]{0,1:T(8,128)S(1)}, u32[]{:S(2)}) copy-start(f32[8,64]{0,1:T(8,128)S(1)} %get-tuple-element.404) | copy-start | bytes 6148
  217.6 4.9 %copy-start.11 = (f32[8,64,512]{2,0,1:T(8,128)}, f32[8,64,512]{2,0,1:T(8,128)S(1)}, u32[]{:S(2)}) copy-start(f32[8,64,512]{2,0,1:T(8,128)S(1)} %get-tuple-element.407) | copy-start | bytes 3145732
  217.6 41.3 %copy-start.22 = (f32[8,64]{0,1:T(8,128)}, f32[8,64]{0,1:T(8,128)S(1)}, u32[]{:S(2)}) copy-start(f32[8,64]{0,1:T(8,128)S(1)} %get-tuple-element.406) | copy-start | bytes 6148
  310.2 3.9 %copy-start.6 = (f32[8,64,512]{2,0,1:T(8,128)S(1)}, f32[8,64,512]{2,0,1:T(8,128)}, u32[]{:S(2)}) copy-start(f32[8,64,512]{2,0,1:T(8,128)} %copy-done.5) | copy-start | bytes 3145732
  310.2 3.9 %copy-start.17 = (f32[8,64]{0,1:T(8,128)S(1)}, f32[8,64]{0,1:T(8,128)}, u32[]{:S(2)}) copy-start(f32[8,64]{0,1:T(8,128)} %copy-done.16) | copy-start | bytes 6148
  310.2 5.1 %copy-start.8 = (f32[8,64,512]{2,0,1:T(8,128)S(1)}, f32[8,64,512]{2,0,1:T(8,128)}, u32[]{:S(2)}) copy-start(f32[8,64,512]{2,0,1:T(8,128)} %copy-done.7) | copy-start | bytes 3145732
  310.2 5.1 %copy-start.19 = (f32[8,64]{0,1:T(8,128)S(1)}, f32[8,64]{0,1:T(8,128)}, u32[]{:S(2)}) copy-start(f32[8,64]{0,1:T(8,128)} %copy-done.18) | copy-start | bytes 6148
  311.6 5.1 %copy-start.10 = (f32[8,64,512]{2,0,1:T(8,128)S(1)}, f32[8,64,512]{2,0,1:T(8,128)}, u32[]{:S(2)}) copy-start(f32[8,64,512]{2,0,1:T(8,128)} %copy-done.9) | copy-start | bytes 3145732
  311.6 5.1 %copy-start.21 = (f32[8,64]{0,1:T(8,128)S(1)}, f32[8,64]{0,1:T(8,128)}, u32[]{:S(2)}) copy-start(f32[8,64]{0,1:T(8,128)} %copy-done.20) | copy-start | bytes 6148
  312.8 5.1 %copy-start.12 = (f32[8,64,512]{2,0,1:T(8,128)S(1)}, f32[8,64,512]{2,0,1:T(8,128)}, u32[]{:S(2)}) copy-start(f32[8,64,512]{2,0,1:T(8,128)} %copy-done.11) | copy-start | bytes 3145732
  312.8 5.1 %copy-start.23 = (f32[8,64]{0,1:T(8,128)S(1)}, f32[8,64]{0,1:T(8,128)}, u32[]{:S(2)}) copy-start(f32[8,64]{0,1:T(8,128)} %copy-done.22) | copy-start | bytes 6148
  323.1 4.8 %collective-permute-start = (f32[8,3]{1,0:T(8,128)S(1)}, f32[8,3]{1,0:T(8,128)S(1)}, u32[]{:S(2)}, u32[]{:S(2)}) collective-permute-start(f32[8,3]{1,0:T(8,128)S(1)} %get-tuple-element.388), channel_id=1, source_target_pairs={{0,8},{8,16},{16,24},{24,32},{32,40},{40,48},{48,56},{56,64},{64,7... | collective-permute-start | bytes 296 | tf_op jit(solution)/shard_map/ppermute | solution.py:33
  325.9 4.9 %collective-permute-start.1 = (f32[8,3]{1,0:T(8,128)S(1)}, f32[8,3]{1,0:T(8,128)S(1)}, u32[]{:S(2)}, u32[]{:S(2)}) collective-permute-start(f32[8,3]{1,0:T(8,128)S(1)} %get-tuple-element.389), channel_id=1, source_target_pairs={{8,0},{16,8},{24,16},{32,24},{40,32},{48,40},{56,48},{64,56},{72,6... | collective-permute-start | bytes 296 | tf_op jit(solution)/shard_map/ppermute | solution.py:35
  (5 other events, 8.9 us)
Sparse Core Ops, SparseCore 0:
  10.6 53.0 all-gather.8
  65.5 53.6 all-gather.4
  150.1 54.3 all-gather.6
where the time goes:
time: 343 us; the launch traced here: 338 us
  waiting for transfers between devices  109 us (32%)
  local copies, waits for them, and re-layouts  65.4 us (19%)
  other arithmetic  54.6 us (16%)
  blocking collectives  47.3 us (14%)
  matrix products  22.9 us (7%)
  starting transfers between devices  21.8 us (6%)
  between operations  15.1 us (4%)
    all_gather x1, waiting for transfers between devices, on_device(): lax.all_gather(decode_queries[0], 'ctx', axis=1, tiled=True)  50.1 us
    all_gather x2, blocking collectives, combined_all(): gathered = jax.tree.map(lambda a: lax.all_gather(a, axis), part)  47.3 us
    all_to_all x1, waiting for transfers between devices, on_device(): lax.all_to_all(cache_acc[None], 'ctx', split_axis=2, concat_axis=0, tiled...  29.2 us
    add x31, other arithmetic, merge_stats(): earlier[1] * jnp.exp(earlier[0] - highest)  25.3 us
    all_gather x1, waiting for transfers between devices, on_device(): lax.all_gather(window_local, 'ctx', axis=1, tiled=True)  19 us
    unnamed x87, local copies, waits for them, and re-layouts  13.2 us
    another operation x2, local copies, waits for them, and re-layouts, on_device(): cache_acc[None]  11.9 us
    dot_general x8, matrix products, on_device(): jnp.einsum('wgd,td->gwt', head_queries, key_head_rows, preferred_element_...  11.5 us
  transfers between devices with their start and end apart: 8, of which 5 were waited for; matrix products, arithmetic and copies ran while one was open for 21% of the time, Pallas kernels for 0%

commit v1 on v0

v1 whole, which is shorter than its diff:
```python
import math

import jax
import jax.numpy as jnp
import numpy as np
from jax import lax
from jax.experimental import pallas as pl
from jax.experimental.pallas import tpu as pltpu
from jax.sharding import PartitionSpec as P

MESH = pl.DeviceIdType.MESH
F32 = jnp.float32
BF16 = jnp.bfloat16
KEY_HEADS = 8
HEAD_DIMENSION = 128
BLOCK = 128
POOL = 7
WIN = 64
STEPS = 4
CHIPS = 16
GROUPS = 8
POSITIONS = 512
SPAN = 2 * POSITIONS
EDGE = 16
ROWS = SPAN + 2 * EDGE
PIECE = 96
NPIECE = ROWS // PIECE
KV_ROWS = 2 * BLOCK + 16
QT_ROWS = 192
LOW = -1e30
SCALE = 1.0 / math.sqrt(HEAD_DIMENSION)
NT = (((1,), (1,)), ((), ()))


def rotary_table():
    exponent = np.arange(0, HEAD_DIMENSION, 2).astype(np.float32) / np.float32(HEAD_DIMENSION)
    inverse = np.power(np.float32(500000.0), -exponent).astype(np.float32)
    wavelength = np.float32(2.0 * math.pi) / inverse
    smooth = (np.float32(8192.0) / wavelength - np.float32(1.0)) / np.float32(3.0)
    blended = (np.float32(1.0) - smooth) * inverse / np.float32(8.0) + smooth * inverse
    adjusted = np.where(
        wavelength > 8192.0,
        inverse / np.float32(8.0),
        np.where(wavelength < 2048.0, inverse, blended),
    ).astype(np.float32)
    start = 2 * CHIPS * POSITIONS - WIN
    positions = (np.arange(WIN) + start).astype(np.float32)
    angles = (positions[:, None] * adjusted[None, :]).astype(np.float32).astype(np.float64)
    cosine, sine = np.cos(angles), np.sin(angles)
    return (
        np.concatenate([cosine, cosine], axis=1).astype(np.float32),
        np.concatenate([-sine, sine], axis=1).astype(np.float32),
    )


def dot(a, b):
    return jnp.dot(a, b, preferred_element_type=F32)


def dot_nt(a, b):
    return lax.dot_general(a, b, NT, preferred_element_type=F32)


def body(
    states,
    weight,
    keys,
    values,
    kept,
    counts,
    queries,
    tail_keys,
    tail_values,
    lengths,
    cosine,
    sine,
    votes_out,
    decode_out,
    w_both,
    keys_own,
    values_own,
    keys_span,
    gathered,
    partial,
    parts,
    window,
    exps,
    stat,
    stat_in,
    total,
    total_in,
    columns,
    pooled,
    pooled_in,
    kv_out,
    kv_in,
    qt_out,
    qt_in,
    dec_scores,
    tail_scores,
    dec_send,
    dec_in,
    local_sem,
    piece_send,
    piece_recv,
    gather_send,
    gather_recv,
    pair_send,
    pair_recv,
    part_send,
    part_recv,
    window_send,
    window_recv,
    stat_send,
    stat_recv,
    total_send,
    total_recv,
    kv_send,
    kv_recv,
    fwd_send,
    fwd_recv,
    qt_send,
    qt_recv,
    dec_send_sem,
    dec_recv,
):
    c = lax.axis_index("ctx")
    z = lax.axis_index("grp")
    p = c // 2
    j = c % 2
    sibling = 2 * p + (1 - j)
    half = p // 8
    slot = p % 8

    def remote(src, dst, send_sem, recv_sem, ctx, grp):
        return pltpu.make_async_remote_copy(
            src_ref=src,
            dst_ref=dst,
            send_sem=send_sem,
            recv_sem=recv_sem,
            device_id=(ctx, grp),
            device_id_type=MESH,
        )

    def core_of(chip):
        return 2 * chip + j

    def each(low, high, step):
        def go(i, carry):
            step(i)
            return carry

        lax.fori_loop(low, high, go, 0)

    own_rows = pl.ds(pl.multiple_of(EDGE + j * POSITIONS, 16), POSITIONS)
    load_w = pltpu.make_async_copy(weight, w_both.at[j], local_sem.at[0])
    load_k = pltpu.make_async_copy(keys.at[0], keys_own, local_sem.at[1])
    load_v = pltpu.make_async_copy(values.at[0], values_own, local_sem.at[2])
    load_span = pltpu.make_async_copy(keys.at[0], keys_span.at[own_rows], local_sem.at[3])
    row0 = pl.multiple_of(32 * j + 16 * (p // 8), 16)

    def piece_of(g):
        col0 = pl.multiple_of(g * 1024 + 128 * (p % 8), 128)
        return states.at[0, pl.ds(row0, 16), pl.ds(col0, 128)]

    load_piece = pltpu.make_async_copy(piece_of(z), gathered.at[p, z], local_sem.at[4])

    def qt_load(k):
        cols = pl.ds(pl.multiple_of(k * 128, 128), 128)
        return (
            pltpu.make_async_copy(
                tail_keys.at[0, 0, :, cols], qt_out.at[k, pl.ds(0, 64)], local_sem.at[8 + k]
            ),
            pltpu.make_async_copy(
                tail_values.at[0, 0, :, cols], qt_out.at[k, pl.ds(64, 64)], local_sem.at[16 + k]
            ),
            pltpu.make_async_copy(
                queries.at[k], qt_out.at[k, pl.ds(128, 32)], local_sem.at[24 + k]
            ),
        )

    load_piece.start()
    load_k.start()
    load_v.start()
    load_w.start()
    load_span.start()

    def qt_start(k):
        for copy in qt_load(k):
            copy.start()

    each(0, KEY_HEADS, qt_start)

    barrier = pltpu.get_barrier_semaphore()

    def greet(ctx, grp):
        pl.semaphore_signal(barrier, inc=1, device_id=(ctx, grp), device_id_type=MESH)

    each(1, CHIPS, lambda d: greet(core_of(lax.rem(p + d, CHIPS)), z))
    greet(sibling, z)

    def greet_group(d):
        g = lax.rem(z + d, GROUPS)
        greet(c, g)
        greet(sibling, g)

    each(1, GROUPS, greet_group)
    pl.semaphore_wait(barrier, CHIPS - 1 + 1 + 2 * (GROUPS - 1))

    def piece_copy(g_to, slot_of):
        return remote(
            piece_of(g_to),
            gathered.at[p, slot_of],
            piece_send.at[g_to],
            piece_recv.at[slot_of],
            c,
            g_to,
        )

    each(1, GROUPS, lambda d: piece_copy(lax.rem(z + d, GROUPS), z).start())

    share_w = remote(weight, w_both.at[j], pair_send.at[0], pair_recv.at[0], sibling, z)
    share_k = remote(keys.at[0], keys_span.at[own_rows], pair_send.at[1], pair_recv.at[1], sibling, z)
    share_w.start()
    share_k.start()

    load_piece.wait()
    each(
        1,
        GROUPS,
        lambda d: piece_copy(
            lax.rem(z + GROUPS - d, GROUPS), lax.rem(z + GROUPS - d, GROUPS)
        ).wait_recv(),
    )

    def gather_copy(chip, source):
        return remote(
            gathered.at[source],
            gathered.at[source],
            gather_send.at[chip],
            gather_recv.at[source],
            core_of(chip),
            z,
        )

    each(1, CHIPS, lambda d: gather_copy(lax.rem(p + d, CHIPS), p).start())

    load_k.wait()
    load_v.wait()

    def kv_copy(k, side):
        chip = k + 8 * side
        return remote(
            kv_out.at[k],
            kv_in.at[j * CHIPS + p],
            kv_send.at[chip],
            kv_recv.at[p],
            core_of(chip),
            z,
        )

    kv_self = pltpu.make_async_copy(kv_out.at[slot], kv_in.at[j * CHIPS + p], local_sem.at[5])
    for k in range(KEY_HEADS):
        cols = slice(k * 128, (k + 1) * 128)
        block = kept[0, k, 0] - c * (POSITIONS // BLOCK)
        chosen = [
            jnp.where(jnp.full((BLOCK, 128), block, jnp.int32) == b, 1.0, 0.0).astype(BF16)
            for b in range(POSITIONS // BLOCK)
        ]
        for n, own in ((0, keys_own), (1, values_own)):
            kv_out[k, n * BLOCK : (n + 1) * BLOCK, :] = sum(
                chosen[b] * own[b * BLOCK : (b + 1) * BLOCK, cols]
                for b in range(POSITIONS // BLOCK)
            )
        live = jnp.full((16, 128), counts[0, k, 0], jnp.int32) > 0
        kv_out[k, 2 * BLOCK : KV_ROWS, :] = jnp.where(live, 0.0, LOW).astype(BF16)
        for side in range(2):

            @pl.when(k + 8 * side != p)
            def _():
                kv_copy(k, side).start()

    kv_self.start()

    step_row = lax.broadcasted_iota(jnp.int32, (32, 128), 0) // 8
    lane = lax.broadcasted_iota(jnp.int32, (32, 128), 1)
    tail_bias = jnp.where(lane < lengths[0, 0] + step_row, 0.0, LOW).astype(BF16)

    def qt_copy(k):
        return remote(
            qt_out.at[k],
            qt_in.at[slot],
            qt_send.at[k],
            qt_recv.at[slot],
            core_of(8 * half + k),
            z,
        )

    def qt_go(k):
        for copy in qt_load(k):
            copy.wait()
        qt_out[k, 160:QT_ROWS, :] = tail_bias

        @pl.when(k != slot)
        def _():
            qt_copy(k).start()

    each(0, KEY_HEADS, qt_go)
    qt_self = pltpu.make_async_copy(qt_out.at[slot], qt_in.at[slot], local_sem.at[6])
    qt_self.start()

    load_w.wait()
    share_w.wait_recv()
    each(
        1,
        CHIPS,
        lambda d: gather_copy(
            lax.rem(p + CHIPS - d, CHIPS), lax.rem(p + CHIPS - d, CHIPS)
        ).wait_recv(),
    )
    for core in range(2):
        for i in range(2):
            acc = jnp.zeros((128, 256), F32)
            for m in range(4):
                left = gathered[8 * i + 2 * m].reshape(128, 128)
                right = gathered[8 * i + 2 * m + 1].reshape(128, 128)
                acc = acc + dot(
                    jnp.concatenate([left, right], axis=1),
                    w_both[core, 256 * m : 256 * (m + 1), :],
                )
            partial[core, :, 16 * i : 16 * (i + 1), :] = acc.reshape(GROUPS, 16, 256)

    def part_copy(core, g_to, g_from, j_from):
        return remote(
            partial.at[core, g_to],
            parts.at[g_from, j_from],
            part_send.at[core, g_to],
            part_recv.at[g_from, j_from],
            2 * p + core,
            g_to,
        )

    def part_go(d):
        g = lax.rem(z + d, GROUPS)
        part_copy(0, g, z, j).start()
        part_copy(1, g, z, j).start()

    each(1, GROUPS, part_go)
    part_copy(1 - j, z, z, j).start()
    parts[z, j] = partial[j, z]

    load_span.wait()
    share_k.wait_recv()

    def edge_copy(up):
        src = keys_span.at[pl.ds(SPAN if up else EDGE, EDGE)]
        dst = keys_span.at[pl.ds(0 if up else SPAN + EDGE, EDGE)]
        chip = p + 1 if up else p - 1
        n = 2 + int(up)
        return remote(src, dst, pair_send.at[n], pair_recv.at[n], core_of(chip), z)

    @pl.when(p < CHIPS - 1)
    def _():
        edge_copy(True).start()

    @pl.when(p > 0)
    def _():
        edge_copy(False).start()

    @pl.when(p == 0)
    def _():
        keys_span[0:EDGE, :] = jnp.zeros((EDGE, 1024), BF16)

    @pl.when(p == CHIPS - 1)
    def _():
        keys_span[SPAN + EDGE : ROWS, :] = jnp.zeros((EDGE, 1024), BF16)

    kv_self.wait()

    def kv_wait(source):
        @pl.when(source != p)
        def _():
            remote(
                kv_in.at[j * CHIPS + source],
                kv_in.at[j * CHIPS + source],
                kv_send.at[0],
                kv_recv.at[source],
                core_of(source),
                z,
            ).wait_recv()

    def fwd_copy(n, core):
        part = kv_in.at[pl.ds(core * CHIPS + 4 * n, 4)]
        return remote(part, part, fwd_send.at[n], fwd_recv.at[n], sibling, z)

    def fwd_go(n):
        each(4 * n, 4 * n + 4, kv_wait)
        fwd_copy(n, j).start()

    each(0, 4, fwd_go)

    def part_wait(d):
        g = lax.rem(z + GROUPS - d, GROUPS)
        part_copy(0, g, g, 0).wait_recv()
        part_copy(0, g, g, 1).wait_recv()

    each(1, GROUPS, part_wait)
    part_copy(0, z, z, 1 - j).wait_recv()
    for i in range(2):
        summed = parts[0, i]
        for g in range(1, GROUPS):
            summed = summed + parts[g, i]
        turn_c = cosine[32 * i : 32 * (i + 1), :]
        turn_s = sine[32 * i : 32 * (i + 1), :]
        for h in range(2):
            head = summed[:, 128 * h : 128 * (h + 1)]
            turned = head * turn_c + pltpu.roll(head, 64, axis=1) * turn_s
            window[p, h, 32 * i : 32 * (i + 1), :] = turned.astype(BF16)

    def window_copy(chip, source):
        return remote(
            window.at[source],
            window.at[source],
            window_send.at[chip],
            window_recv.at[source],
            core_of(chip),
            z,
        )

    each(1, CHIPS, lambda d: window_copy(lax.rem(p + d, CHIPS), p).start())

    qt_self.wait()

    def qt_wait(r):
        @pl.when(r != slot)
        def _():
            remote(
                qt_in.at[r], qt_in.at[r], qt_send.at[0], qt_recv.at[r], core_of(8 * half + r), z
            ).wait_recv()

    each(0, 8, qt_wait)
    each(0, 4, lambda n: fwd_copy(n, 1 - j).wait_recv())
    rows_q = qt_in[:, 128:160, :].reshape(256, 128)

    def tail_go(r):
        s = dot_nt(qt_in[r, 128:160, :], qt_in[r, 0:128, :]) * SCALE
        tail_scores[r] = s + qt_in[r, 160:QT_ROWS, :].astype(F32)

    each(0, 8, tail_go)
    top = tail_scores[...].reshape(256, 128)

    def score_go(b, top):
        s = dot_nt(rows_q, kv_in[b, 0:BLOCK, :]) * SCALE
        s = s + kv_in[b, 2 * BLOCK : KV_ROWS, :].astype(F32)[0:1, :]
        dec_scores[b] = s
        return jnp.maximum(top, s)

    top = lax.fori_loop(0, 2 * CHIPS, score_go, top)
    top = jnp.max(top, axis=1, keepdims=True)

    def split(weights):
        high = weights.astype(BF16)
        return high, (weights - high.astype(F32)).astype(BF16)

    tail_weights = jnp.exp(tail_scores[...].reshape(256, 128) - top)
    tail_acc = []
    for r in range(8):
        high, low = split(tail_weights[32 * r : 32 * (r + 1), :])
        right = qt_in[r, 64:QT_ROWS, :]
        tail_acc.append(dot(high, right) + dot(low, right))

    def value_go(b, carry):
        acc, weight_sum = carry
        weights = jnp.exp(dec_scores[b] - top)
        high, low = split(weights)
        right = kv_in[b, BLOCK : 2 * BLOCK, :]
        both = dot(jnp.concatenate([high, low], axis=1), jnp.concatenate([right, right], axis=0))
        return acc + both, weight_sum + weights

    acc, weight_sum = lax.fori_loop(
        0, 2 * CHIPS, value_go, (jnp.concatenate(tail_acc, axis=0), tail_weights)
    )
    result = acc / jnp.sum(weight_sum, axis=1, keepdims=True)
    dec_send[...] = result.astype(BF16).reshape(8, 32, 128)

    def dec_copy(r):
        return remote(
            dec_send.at[r],
            dec_in.at[slot],
            dec_send_sem.at[r],
            dec_recv.at[slot],
            core_of(8 * half + r),
            z,
        )

    def dec_go(r):
        @pl.when(r != slot)
        def _():
            dec_copy(r).start()

    each(0, 8, dec_go)
    dec_self = pltpu.make_async_copy(dec_send.at[slot], dec_in.at[slot], local_sem.at[7])
    dec_self.start()

    @pl.when(p > 0)
    def _():
        edge_copy(True).wait_recv()

    @pl.when(p < CHIPS - 1)
    def _():
        edge_copy(False).wait_recv()

    piece_row = lax.broadcasted_iota(jnp.int32, (PIECE, 256), 0)
    piece_lane = lax.broadcasted_iota(jnp.int32, (PIECE, 256), 1)
    hidden_first = jnp.logical_and(piece_row < EDGE, p == 0)
    last_row = piece_row + (NPIECE - 1) * PIECE
    hidden_last = jnp.logical_or(
        jnp.logical_and(last_row >= SPAN + EDGE, p == CHIPS - 1),
        jnp.logical_and(
            last_row < SPAN + EDGE,
            p * SPAN + last_row - EDGE
            > (2 * CHIPS * POSITIONS - WIN) + jnp.bitwise_and(piece_lane, WIN - 1),
        ),
    )

    def stat_copy(o):
        return remote(
            stat.at[o], stat_in.at[p], stat_send.at[o], stat_recv.at[p], core_of(o), z
        )

    def window_go(k):
        for n in range(2):
            source = 2 * k + n

            @pl.when(source != p)
            def _():
                window_copy(0, source).wait_recv()

        rows = window[pl.ds(2 * k, 2)].reshape(256, 128)
        cols = pl.ds(pl.multiple_of(k * 128, 128), 128)
        top = jnp.full((8, 256), LOW, F32)
        for i in range(NPIECE):
            s = dot_nt(keys_span[PIECE * i : PIECE * (i + 1), cols], rows) * SCALE
            if i == 0:
                s = jnp.where(hidden_first, LOW, s)
            if i == NPIECE - 1:
                s = jnp.where(hidden_last, LOW, s)
            exps[k, PIECE * i : PIECE * (i + 1), :] = s
            top = jnp.maximum(top, jnp.max(s.reshape(PIECE // 8, 8, 256), axis=0))
        top = jnp.max(top, axis=0, keepdims=True)
        summed = jnp.zeros((8, 256), F32)
        for i in range(NPIECE):
            e = jnp.exp(exps[k, PIECE * i : PIECE * (i + 1), :] - top)
            exps[k, PIECE * i : PIECE * (i + 1), :] = e
            if i == 0:
                e = e[EDGE:]
            if i == NPIECE - 1:
                e = e[: PIECE - EDGE]
            summed = summed + jnp.sum(e.reshape(-1, 8, 256), axis=0)
        summed = jnp.sum(summed, axis=0, keepdims=True)
        for n in range(2):
            o = 2 * k + n
            stat[o, 0:1, :] = top[:, 128 * n : 128 * (n + 1)]
            stat[o, 1:2, :] = summed[:, 128 * n : 128 * (n + 1)]

            @pl.when(o != p)
            def _():
                stat_copy(o).start()

    each(0, KEY_HEADS, window_go)
    stat_in[p] = stat[p]

    def stat_wait(d):
        source = lax.rem(p + CHIPS - d, CHIPS)
        remote(
            stat.at[source], stat_in.at[source], stat_send.at[0], stat_recv.at[source], core_of(source), z
        ).wait_recv()

    each(1, CHIPS, stat_wait)
    peak = stat_in[0, 0:1, :]
    for o in range(1, CHIPS):
        peak = jnp.maximum(peak, stat_in[o, 0:1, :])
    merged = jnp.zeros((1, 128), F32)
    for o in range(CHIPS):
        merged = merged + stat_in[o, 1:2, :] * jnp.exp(stat_in[o, 0:1, :] - peak)
    total[0:1, :] = peak
    total[1:2, :] = merged

    def total_copy(chip, source):
        return remote(
            total, total_in.at[source], total_send.at[chip], total_recv.at[source], core_of(chip), z
        )

    each(1, CHIPS, lambda d: total_copy(lax.rem(p + d, CHIPS), p).start())
    total_in[p] = total[...]

    dec_self.wait()

    def dec_wait(k):
        @pl.when(k != slot)
        def _():
            remote(
                dec_send.at[k], dec_in.at[k], dec_send_sem.at[0], dec_recv.at[k], core_of(8 * half + k), z
            ).wait_recv()

    each(0, 8, dec_wait)
    decode_out[...] = dec_in[...]

    each(
        1,
        CHIPS,
        lambda d: total_copy(
            lax.rem(p + CHIPS - d, CHIPS), lax.rem(p + CHIPS - d, CHIPS)
        ).wait_recv(),
    )

    factors = []
    for o in range(CHIPS):
        factors.append(
            jnp.exp(stat[o, 0:1, :] - total_in[o, 0:1, :]) / total_in[o, 1:2, :]
        )
    head_lane = lax.broadcasted_iota(jnp.int32, (PIECE, 128), 1)
    for i in range(NPIECE):
        rows = slice(PIECE * i, PIECE * (i + 1))
        votes = jnp.zeros((PIECE, 128), F32)
        for k in range(KEY_HEADS):
            weighted = (
                exps[k, rows, 0:128] * factors[2 * k] + exps[k, rows, 128:256] * factors[2 * k + 1]
            )
            votes = jnp.where(head_lane == k, jnp.sum(weighted, axis=1, keepdims=True), votes)
        columns[rows, :] = votes
    columns[ROWS:, :] = jnp.zeros((columns.shape[0] - ROWS, 128), F32)
    lanes = columns.shape[0]
    across = jnp.transpose(columns[...])[0:KEY_HEADS, :]
    near = POOL // 2
    window_sum = jnp.zeros((KEY_HEADS, lanes), F32)
    for shift in range(EDGE - near, EDGE + near + 1):
        window_sum = window_sum + pltpu.roll(across, lanes - shift, axis=1)
    for n in range(2):
        pooled[n] = window_sum[:, POSITIONS * n : POSITIONS * (n + 1)]
    share_votes = remote(pooled.at[1 - j], pooled_in, pair_send.at[4], pair_recv.at[4], sibling, z)
    share_votes.start()
    share_votes.wait_recv()
    votes_out[...] = (pooled[j] + pooled_in[...]) * (
        2 * CHIPS * POSITIONS / (WIN * 8) / POOL
    )

    share_votes.wait_send()
    share_w.wait_send()
    share_k.wait_send()

    @pl.when(p < CHIPS - 1)
    def _():
        edge_copy(True).wait_send()

    @pl.when(p > 0)
    def _():
        edge_copy(False).wait_send()

    def sent_group(d):
        g = lax.rem(z + d, GROUPS)
        piece_copy(g, z).wait_send()
        part_copy(0, g, z, j).wait_send()
        part_copy(1, g, z, j).wait_send()

    each(1, GROUPS, sent_group)
    part_copy(1 - j, z, z, j).wait_send()

    def sent_chip(d):
        chip = lax.rem(p + d, CHIPS)
        gather_copy(chip, p).wait_send()
        window_copy(chip, p).wait_send()
        stat_copy(chip).wait_send()
        total_copy(chip, p).wait_send()
        kv_copy(chip % 8, chip // 8).wait_send()

    each(1, CHIPS, sent_chip)
    each(0, 4, lambda n: fwd_copy(n, j).wait_send())

    def sent_slot(k):
        @pl.when(k != slot)
        def _():
            qt_copy(k).wait_send()
            dec_copy(k).wait_send()

    each(0, 8, sent_slot)


def on_device(
    window_states,
    query_weight,
    cache_keys,
    cache_values,
    kept_blocks,
    retained_block_count,
    decode_queries,
    tail_keys,
    tail_values,
    row_lengths,
):
    cosine, sine = rotary_table()
    queries = (
        decode_queries.reshape(STEPS, KEY_HEADS, 8, HEAD_DIMENSION)
        .transpose(1, 0, 2, 3)
        .reshape(KEY_HEADS, 32, HEAD_DIMENSION)
    )
    hbm = pl.BlockSpec(memory_space=pl.ANY)
    smem = pl.BlockSpec(memory_space=pltpu.SMEM)
    vmem = pl.BlockSpec(memory_space=pltpu.VMEM)
    dma = pltpu.SemaphoreType.DMA
    votes, decoded = pl.pallas_call(
        body,
        out_shape=(
            jax.ShapeDtypeStruct((KEY_HEADS, POSITIONS), F32),
            jax.ShapeDtypeStruct((KEY_HEADS, 32, HEAD_DIMENSION), BF16),
        ),
        in_specs=[hbm, hbm, hbm, hbm, smem, smem, hbm, hbm, hbm, smem, vmem, vmem],
        out_specs=(vmem, vmem),
        scratch_shapes=[
            pltpu.VMEM((2, 1024, 256), BF16),
            pltpu.VMEM((POSITIONS, 1024), BF16),
            pltpu.VMEM((POSITIONS, 1024), BF16),
            pltpu.VMEM((ROWS, 1024), BF16),
            pltpu.VMEM((CHIPS, GROUPS, 16, 128), BF16),
            pltpu.VMEM((2, GROUPS, 32, 256), F32),
            pltpu.VMEM((GROUPS, 2, 32, 256), F32),
            pltpu.VMEM((CHIPS, 2, WIN, 128), BF16),
            pltpu.VMEM((KEY_HEADS, ROWS, 256), F32),
            pltpu.VMEM((CHIPS, 2, 128), F32),
            pltpu.VMEM((CHIPS, 2, 128), F32),
            pltpu.VMEM((2, 128), F32),
            pltpu.VMEM((CHIPS, 2, 128), F32),
            pltpu.VMEM((ROWS + 96, 128), F32),
            pltpu.VMEM((2, KEY_HEADS, POSITIONS), F32),
            pltpu.VMEM((KEY_HEADS, POSITIONS), F32),
            pltpu.VMEM((KEY_HEADS, KV_ROWS, 128), BF16),
            pltpu.VMEM((2 * CHIPS, KV_ROWS, 128), BF16),
            pltpu.VMEM((KEY_HEADS, QT_ROWS, 128), BF16),
            pltpu.VMEM((8, QT_ROWS, 128), BF16),
            pltpu.VMEM((2 * CHIPS, 256, 128), F32),
            pltpu.VMEM((8, 32, 128), F32),
            pltpu.VMEM((8, 32, 128), BF16),
            pltpu.VMEM((8, 32, 128), BF16),
            dma((32,)),
            dma((GROUPS,)),
            dma((GROUPS,)),
            dma((CHIPS,)),
            dma((CHIPS,)),
            dma((5,)),
            dma((5,)),
            dma((2, GROUPS)),
            dma((GROUPS, 2)),
            dma((CHIPS,)),
            dma((CHIPS,)),
            dma((CHIPS,)),
            dma((CHIPS,)),
            dma((CHIPS,)),
            dma((CHIPS,)),
            dma((CHIPS,)),
            dma((CHIPS,)),
            dma((4,)),
            dma((4,)),
            dma((8,)),
            dma((8,)),
            dma((8,)),
            dma((8,)),
        ],
        compiler_params=pltpu.CompilerParams(
            collective_id=0, has_side_effects=True, vmem_limit_bytes=48 * 1024 * 1024
        ),
        cost_estimate=pl.CostEstimate(
            flops=1_400_000_000, bytes_accessed=6_000_000, transcendentals=3_500_000
        ),
    )(
        window_states,
        query_weight,
        cache_keys,
        cache_values,
        kept_blocks,
        retained_block_count,
        queries,
        tail_keys,
        tail_values,
        row_lengths,
        jnp.asarray(cosine),
        jnp.asarray(sine),
    )
    decoded = (
        decoded.reshape(KEY_HEADS, STEPS, 8, HEAD_DIMENSION)
        .transpose(1, 0, 2, 3)
        .reshape(1, STEPS, 1, KEY_HEADS * 8 * HEAD_DIMENSION)
    )
    return votes[None], decoded


def solution(mesh):
    placed = (
        P("grp", None, None),
        P("grp", "ctx"),
        P("grp", "ctx", None),
        P("grp", "ctx", None),
        P("grp", None, "ctx"),
        P("grp", None, "ctx"),
        P("grp", None, "ctx", None),
        P("grp", "ctx", None, None),
        P("grp", "ctx", None, None),
        P("grp", "ctx"),
    )
    return jax.shard_map(
        on_device,
        mesh=mesh,
        in_specs=placed,
        out_specs=(P("grp", None, "ctx"), P("grp", None, "ctx", None)),
        check_vma=False,
    )
```

time: 343 us -> 91.4 us (0.27); the launches traced: 338 us -> 90.9 us
  waiting for transfers between devices: 109 us -> 0 us
  Pallas kernels: 0 us -> 78.8 us
  local copies, waits for them, and re-layouts: 65.4 us -> 10.7 us
  other arithmetic: 54.6 us -> 0 us
  blocking collectives: 47.3 us -> 0 us
  matrix products: 22.9 us -> 0 us
  starting transfers between devices: 21.8 us -> 0 us
  between operations: 15.1 us -> 1.36 us
    pallas_call x0 -> x1, Pallas kernels: none -> 78.8 us  [on_device(): pl.pallas_call(body, out_shape=(jax.ShapeDtypeStruct((KEY_HEADS, POSITION...]
    all_gather x3 -> x0, waiting for transfers between devices: 69.1 us -> none  [the longest x1 50.1 us: on_device(): lax.all_gather(decode_queries[0], 'ctx', axis=1, tiled=True)]
    all_gather x2 -> x0, blocking collectives: 47.3 us -> none  [combined_all(): gathered = jax.tree.map(lambda a: lax.all_gather(a, axis), part)]
    all_to_all x3 -> x0, waiting for transfers between devices: 35.5 us -> none  [the longest x1 29.2 us: on_device(): lax.all_to_all(cache_acc[None], 'ctx', split_axis=2, concat_axis=0, tiled...]
    add x36 -> x0, other arithmetic: 25.3 us -> none  [the longest x31 25.3 us: merge_stats(): earlier[1] * jnp.exp(earlier[0] - highest)]
    dot_general x13 -> x0, matrix products: 22.9 us -> none  [the longest x8 11.5 us: on_device(): jnp.einsum('wgd,td->gwt', head_queries, key_head_rows, preferred_element_...]
    another operation x26 -> x0, local copies, waits for them, and re-layouts: 18.8 us -> none  [the longest x2 11.9 us: on_device(): cache_acc[None]]
    all_to_all x3 -> x0, starting transfers between devices: 16.7 us -> none  [the longest x1 7.68 us: on_device(): lax.all_to_all(cache_acc[None], 'ctx', split_axis=2, concat_axis=0, tiled...]
  transfers between devices with their start and end apart: 8 -> 0, of which waited for: 5 -> 0; matrix products, arithmetic and copies ran while one was open for 21% -> 0% of each run, Pallas kernels for 0% -> 0%
where the time goes in v1:
time: 91.4 us; the launch traced here: 90.9 us
  Pallas kernels  78.8 us (86%)
  local copies, waits for them, and re-layouts  10.7 us (12%)
  between operations  1.36 us (1%)
    pallas_call x1, Pallas kernels, on_device(): pl.pallas_call(body, out_shape=(jax.ShapeDtypeStruct((KEY_HEADS, POSITION...  78.8 us
    unnamed x19, local copies, waits for them, and re-layouts  9.2 us

profile of v1, /device:TPU:1, one launch (start us, length us, event | category | flops | bytes accessed | tf_op | source)
XLA Modules:
  0.0 90.9 jit_solution(16439033864426260960)
XLA Ops:
  0.6 0.0 copy-start.4
  1.3 0.7 copy.15.kept
  2.1 0.7 copy.16.counts
  2.8 0.8 copy_bitcast_fusion.1.queries
  3.6 0.0 copy-done.4
  3.6 0.0 copy-start
  3.7 1.2 %copy-done = bf16[1,64,8192]{2,1,0:T(8,128)(2,1)S(1)} copy-done((bf16[1,64,8192]{2,1,0:T(8,128)(2,1)S(1)}, bf16[1,64,8192]{2,1,0:T(8,128)(2,1)}, u32[]{:S(2)}) %copy-start) | copy-done | bytes 1048600
  4.9 0.0 copy-start.1
  4.9 1.2 %copy-done.1 = bf16[1,512,1024]{2,1,0:T(8,128)(2,1)S(1)} copy-done((bf16[1,512,1024]{2,1,0:T(8,128)(2,1)S(1)}, bf16[1,512,1024]{2,1,0:T(8,128)(2,1)}, u32[]{:S(2)}) %copy-start.1) | copy-done | bytes 1048600
  6.1 0.0 copy-start.2
  6.1 1.2 %copy-done.2 = bf16[1,512,1024]{2,1,0:T(8,128)(2,1)S(1)} copy-done((bf16[1,512,1024]{2,1,0:T(8,128)(2,1)S(1)}, bf16[1,512,1024]{2,1,0:T(8,128)(2,1)}, u32[]{:S(2)}) %copy-start.2) | copy-done | bytes 1048600
  7.3 0.0 copy-start.3
  7.3 1.0 %copy-done.3 = bf16[1024,256]{1,0:T(8,128)(2,1)S(1)} copy-done((bf16[1024,256]{1,0:T(8,128)(2,1)S(1)}, bf16[1024,256]{1,0:T(8,128)(2,1)}, u32[]{:S(2)}) %copy-start.3) | copy-done | bytes 524312
  8.4 0.0 copy-start.5
  8.4 0.9 copy-done.5
  9.3 0.0 copy-start.6
  9.3 0.8 copy-done.6
  10.0 0.0 copy-start.7
  10.0 0.8 copy-done.7
  10.8 78.8 %shard_map.131 = (f32[8,512]{1,0:T(8,128)S(1)}, bf16[8,32,128]{2,1,0:T(8,128)(2,1)S(1)}) custom-call(bf16[1,64,8192]{2,1,0:T(8,128)(2,1)S(1)} %copy-done, bf16[1024,256]{1,0:T(8,128)(2,1)S(1)} %copy-done.3, bf16[1,512,1024]{2,1,0:T(8,128)(2,1)S(1)} %copy-done.1, bf16[1,512,1024]{2,1,0:T(8,128)(2,1)S(1)} %copy-done.2, s32[1,8,1]{2,1,0:T(8,128)S(1)} %copy.15.kept, ...), custom_call_target="tpu_custom_call" | custom-call | flops 1400000000 | bytes 6000000 | tf_op jit(solution)/shard_map/pallas_call | solution.py:711
  89.6 0.7 reshape.19
  90.3 0.6 copy.24
  (1 shorter events, 0.0 us)
Async XLA Ops:
  0.6 3.0 %copy-start.4 = (bf16[1,1,64,1024]{3,2,1,0:T(8,128)(2,1)S(1)}, bf16[1,1,64,1024]{3,2,1,0:T(8,128)(2,1)}, u32[]{:S(2)}) copy-start(bf16[1,1,64,1024]{3,2,1,0:T(8,128)(2,1)} %tail_keys.1) | copy-start | bytes 393220
  3.6 1.2 %copy-start = (bf16[1,64,8192]{2,1,0:T(8,128)(2,1)S(1)}, bf16[1,64,8192]{2,1,0:T(8,128)(2,1)}, u32[]{:S(2)}) copy-start(bf16[1,64,8192]{2,1,0:T(8,128)(2,1)} %states.1) | copy-start | bytes 3145732
  4.9 1.2 %copy-start.1 = (bf16[1,512,1024]{2,1,0:T(8,128)(2,1)S(1)}, bf16[1,512,1024]{2,1,0:T(8,128)(2,1)}, u32[]{:S(2)}) copy-start(bf16[1,512,1024]{2,1,0:T(8,128)(2,1)} %keys.1) | copy-start | bytes 3145732
  6.1 1.2 %copy-start.2 = (bf16[1,512,1024]{2,1,0:T(8,128)(2,1)S(1)}, bf16[1,512,1024]{2,1,0:T(8,128)(2,1)}, u32[]{:S(2)}) copy-start(bf16[1,512,1024]{2,1,0:T(8,128)(2,1)} %values.1) | copy-start | bytes 3145732
  7.3 1.0 %copy-start.3 = (bf16[1024,256]{1,0:T(8,128)(2,1)S(1)}, bf16[1024,256]{1,0:T(8,128)(2,1)}, u32[]{:S(2)}) copy-start(bf16[1024,256]{1,0:T(8,128)(2,1)} %weight.1) | copy-start | bytes 1572868
  8.4 0.9 copy-start.5
  9.3 0.8 copy-start.6
  10.0 0.8 copy-start.7

commit v2 on v1

v2 whole, which is shorter than its diff:
```python
import math

import jax
import jax.numpy as jnp
import numpy as np
from jax import lax
from jax.experimental import pallas as pl
from jax.experimental.pallas import tpu as pltpu
from jax.sharding import PartitionSpec as P

MESH = pl.DeviceIdType.MESH
F32 = jnp.float32
BF16 = jnp.bfloat16
KEY_HEADS = 8
HEAD_DIMENSION = 128
BLOCK = 128
POOL = 7
WIN = 64
STEPS = 4
CHIPS = 16
GROUPS = 8
PAIRS = GROUPS // 2
POSITIONS = 512
SPAN = 2 * POSITIONS
EDGE = 16
ROWS = SPAN + 2 * EDGE
PIECE = 96
NPIECE = ROWS // PIECE
KV_ROWS = 2 * BLOCK + 16
QT_ROWS = 192
LOW = -1e30
SCALE = 1.0 / math.sqrt(HEAD_DIMENSION)
NT = (((1,), (1,)), ((), ()))


def rotary_table():
    exponent = np.arange(0, HEAD_DIMENSION, 2).astype(np.float32) / np.float32(HEAD_DIMENSION)
    inverse = np.power(np.float32(500000.0), -exponent).astype(np.float32)
    wavelength = np.float32(2.0 * math.pi) / inverse
    smooth = (np.float32(8192.0) / wavelength - np.float32(1.0)) / np.float32(3.0)
    blended = (np.float32(1.0) - smooth) * inverse / np.float32(8.0) + smooth * inverse
    adjusted = np.where(
        wavelength > 8192.0,
        inverse / np.float32(8.0),
        np.where(wavelength < 2048.0, inverse, blended),
    ).astype(np.float32)
    start = 2 * CHIPS * POSITIONS - WIN
    positions = (np.arange(WIN) + start).astype(np.float32)
    angles = (positions[:, None] * adjusted[None, :]).astype(np.float32).astype(np.float64)
    cosine, sine = np.cos(angles), np.sin(angles)
    return np.stack(
        [np.concatenate([cosine, cosine], axis=1), np.concatenate([-sine, sine], axis=1)]
    ).astype(np.float32)


def dot(a, b):
    return jnp.dot(a, b, preferred_element_type=F32)


def dot_nt(a, b):
    return lax.dot_general(a, b, NT, preferred_element_type=F32)


def body(
    states,
    weight,
    keys,
    values,
    kept,
    counts,
    queries,
    tail_keys,
    tail_values,
    lengths,
    turn,
    votes_out,
    decode_out,
    w_all,
    keys_own,
    values_own,
    keys_span,
    gathered,
    partial,
    parts,
    window,
    exps,
    stat,
    stat_in,
    columns,
    pooled,
    pooled_in,
    kv_out,
    kv_in,
    qt_out,
    qt_in,
    dec_scores,
    tail_scores,
    dec_send,
    dec_in,
    kept_own,
    counts_own,
    lengths_own,
    turn_own,
    queries_own,
    local_sem,
    piece_send,
    piece_recv,
    gather_send,
    gather_recv,
    pair_send,
    pair_recv,
    part_send,
    part_recv,
    window_send,
    window_recv,
    stat_send,
    stat_recv,
    weight_send,
    weight_recv,
    kv_send,
    kv_recv,
    fwd_send,
    fwd_recv,
    qt_send,
    qt_recv,
    dec_send_sem,
    dec_recv,
):
    c = lax.axis_index("ctx")
    z = lax.axis_index("grp")
    p = c // 2
    j = c % 2
    sibling = 2 * p + (1 - j)
    half = p // 8
    slot = p % 8

    def remote(src, dst, send_sem, recv_sem, ctx, grp):
        return pltpu.make_async_remote_copy(
            src_ref=src,
            dst_ref=dst,
            send_sem=send_sem,
            recv_sem=recv_sem,
            device_id=(ctx, grp),
            device_id_type=MESH,
        )

    def core_of(chip):
        return 2 * chip + j

    def each(low, high, step):
        def go(i, carry):
            step(i)
            return carry

        lax.fori_loop(low, high, go, 0)

    def every(low, high, step):
        for i in range(low, high):
            step(i)

    side = z % 2
    pair = z // 2
    other = 2 * pair + 1 - side

    barrier = pltpu.get_barrier_semaphore()

    def greet(ctx, grp):
        pl.semaphore_signal(barrier, inc=1, device_id=(ctx, grp), device_id_type=MESH)

    def group_of(d):
        return 2 * lax.rem(pair + d, PAIRS) + side

    for d in range(1, PAIRS):
        greet(c, group_of(d))
        greet(sibling, group_of(d))
    greet(c, other)
    greet(sibling, z)
    every(1, CHIPS, lambda d: greet(core_of(lax.rem(p + d, CHIPS)), z))

    own_rows = pl.ds(pl.multiple_of(EDGE + j * POSITIONS, 16), POSITIONS)
    load_w = pltpu.make_async_copy(weight, w_all.at[side, j], local_sem.at[0])
    load_k = pltpu.make_async_copy(keys.at[0], keys_own, local_sem.at[1])
    load_v = pltpu.make_async_copy(values.at[0], values_own, local_sem.at[2])
    load_span = pltpu.make_async_copy(keys.at[0], keys_span.at[own_rows], local_sem.at[3])
    row0 = pl.multiple_of(32 * j + 16 * (p // 8), 16)

    def piece_of(q):
        col0 = pl.multiple_of(q * 2048 + 256 * (p % 8), 256)
        return states.at[0, pl.ds(row0, 16), pl.ds(col0, 256)]

    load_piece = pltpu.make_async_copy(piece_of(pair), gathered.at[p, pair], local_sem.at[4])
    small = [
        pltpu.make_async_copy(src, dst, local_sem.at[32 + n])
        for n, (src, dst) in enumerate(
            (
                (kept, kept_own),
                (counts, counts_own),
                (lengths, lengths_own),
                (turn, turn_own),
                (queries, queries_own),
            )
        )
    ]

    def qt_load(k):
        cols = slice(k * 128, (k + 1) * 128)
        return (
            pltpu.make_async_copy(
                tail_keys.at[0, 0, :, cols], qt_out.at[k, 0:64], local_sem.at[8 + k]
            ),
            pltpu.make_async_copy(
                tail_values.at[0, 0, :, cols], qt_out.at[k, 64:128], local_sem.at[16 + k]
            ),
        )

    load_k.start()
    load_v.start()
    for copy in small:
        copy.start()
    load_piece.start()
    load_w.start()
    load_span.start()
    for k in range(KEY_HEADS):
        for copy in qt_load(k):
            copy.start()

    for copy in small:
        copy.wait()
    load_k.wait()
    load_v.wait()
    for k in range(KEY_HEADS):
        cols = slice(k * 128, (k + 1) * 128)
        block = jnp.broadcast_to(kept_own[:, k : k + 1], (BLOCK, 128)) - c * (POSITIONS // BLOCK)
        chosen = [
            jnp.where(block == b, 1.0, 0.0).astype(BF16) for b in range(POSITIONS // BLOCK)
        ]
        for n, own in ((0, keys_own), (1, values_own)):
            kv_out[k, n * BLOCK : (n + 1) * BLOCK, :] = sum(
                chosen[b] * own[b * BLOCK : (b + 1) * BLOCK, cols]
                for b in range(POSITIONS // BLOCK)
            )
        live = jnp.broadcast_to(counts_own[:, k : k + 1], (16, 128)) > 0
        kv_out[k, 2 * BLOCK : KV_ROWS, :] = jnp.where(live, 0.0, LOW).astype(BF16)
    step_row = lax.broadcasted_iota(jnp.int32, (32, 128), 0) // 8
    lane = lax.broadcasted_iota(jnp.int32, (32, 128), 1)
    tail_bias = jnp.where(
        lane < jnp.broadcast_to(lengths_own[...], (32, 128)) + step_row, 0.0, LOW
    ).astype(BF16)
    for k in range(KEY_HEADS):
        qt_out[k, 128:160, :] = queries_own[k]
        qt_out[k, 160:QT_ROWS, :] = tail_bias

    pl.semaphore_wait(barrier, CHIPS - 1 + 1 + 2 * (PAIRS - 1) + 1)

    def piece_copy(q_to, q_from):
        return remote(
            piece_of(q_to),
            gathered.at[p, q_from],
            piece_send.at[q_to],
            piece_recv.at[q_from],
            c,
            2 * q_to + side,
        )

    def pair_before(d):
        return lax.rem(pair + PAIRS - d, PAIRS)

    every(1, PAIRS, lambda d: piece_copy(lax.rem(pair + d, PAIRS), pair).start())

    def weight_copy(n):
        rows = pl.ds(512 * n, 512)
        return remote(
            weight.at[rows],
            w_all.at[side, j, rows],
            weight_send.at[n],
            weight_recv.at[n],
            c,
            other,
        )

    def weight_on(n):
        part = w_all.at[1 - side, j, pl.ds(512 * n, 512)]
        return remote(part, part, weight_send.at[2 + n], weight_recv.at[2 + n], sibling, z)

    share_w = remote(weight, w_all.at[side, j], pair_send.at[0], pair_recv.at[0], sibling, z)
    share_k = remote(keys.at[0], keys_span.at[own_rows], pair_send.at[1], pair_recv.at[1], sibling, z)
    weight_copy(0).start()
    weight_copy(1).start()
    share_w.start()

    load_piece.wait()
    every(1, PAIRS, lambda d: piece_copy(pair_before(d), pair_before(d)).wait_recv())

    def gather_copy(chip, source):
        return remote(
            gathered.at[source],
            gathered.at[source],
            gather_send.at[chip],
            gather_recv.at[source],
            core_of(chip),
            z,
        )

    every(1, CHIPS, lambda d: gather_copy(lax.rem(p + d, CHIPS), p).start())
    share_k.start()

    def kv_copy(k, half_to):
        chip = k + 8 * half_to
        return remote(
            kv_out.at[k],
            kv_in.at[j * CHIPS + p],
            kv_send.at[chip],
            kv_recv.at[p],
            core_of(chip),
            z,
        )

    def kv_go(d):
        chip = lax.rem(p + d, CHIPS)
        kv_copy(chip % 8, chip // 8).start()

    kv_self = pltpu.make_async_copy(kv_out.at[slot], kv_in.at[j * CHIPS + p], local_sem.at[5])
    kv_self.start()

    def qt_copy(k):
        return remote(
            qt_out.at[k],
            qt_in.at[slot],
            qt_send.at[k],
            qt_recv.at[slot],
            core_of(8 * half + k),
            z,
        )

    for k in range(KEY_HEADS):
        for copy in qt_load(k):
            copy.wait()

    qt_self = pltpu.make_async_copy(qt_out.at[slot], qt_in.at[slot], local_sem.at[6])
    qt_self.start()

    every(1, CHIPS, kv_go)

    def qt_go(k):
        @pl.when(k != slot)
        def _():
            qt_copy(k).start()

    every(0, KEY_HEADS, qt_go)

    load_w.wait()
    share_w.wait_recv()
    every(
        1,
        CHIPS,
        lambda d: gather_copy(
            lax.rem(p + CHIPS - d, CHIPS), lax.rem(p + CHIPS - d, CHIPS)
        ).wait_recv(),
    )

    def left_of(m):
        return jnp.concatenate(
            [gathered[m].reshape(64, 256), gathered[8 + m].reshape(64, 256)], axis=0
        )

    def product(core, group_side):
        acc = jnp.zeros((128, 256), F32)
        for m in range(4):
            acc = acc + dot(
                left_of(4 * group_side + m), w_all[group_side, core, 256 * m : 256 * (m + 1), :]
            )
        return acc

    for n in range(2):
        weight_copy(n).wait_recv()
        weight_on(n).start()
    for n in range(2):
        weight_on(n).wait_recv()
    for core in range(2):
        acc = (product(core, 0) + product(core, 1)).reshape(2, PAIRS, 16, 256)
        for i in range(2):
            partial[core, :, 16 * i : 16 * (i + 1), :] = acc[i]

    def part_copy(core, q_to, q_from, j_from):
        return remote(
            partial.at[core, q_to],
            parts.at[q_from, j_from],
            part_send.at[core, q_to],
            part_recv.at[q_from, j_from],
            2 * p + core,
            2 * q_to + side,
        )

    for d in range(1, PAIRS):
        q = lax.rem(pair + d, PAIRS)
        part_copy(0, q, pair, j).start()
        part_copy(1, q, pair, j).start()
    part_copy(1 - j, pair, pair, j).start()
    parts[pair, j] = partial[j, pair]

    load_span.wait()
    share_k.wait_recv()

    def edge_copy(up):
        src = keys_span.at[pl.ds(SPAN if up else EDGE, EDGE)]
        dst = keys_span.at[pl.ds(0 if up else SPAN + EDGE, EDGE)]
        chip = p + 1 if up else p - 1
        n = 2 + int(up)
        return remote(src, dst, pair_send.at[n], pair_recv.at[n], core_of(chip), z)

    @pl.when(p < CHIPS - 1)
    def _():
        edge_copy(True).start()

    @pl.when(p > 0)
    def _():
        edge_copy(False).start()

    @pl.when(p == 0)
    def _():
        keys_span[0:EDGE, :] = jnp.zeros((EDGE, 1024), BF16)

    @pl.when(p == CHIPS - 1)
    def _():
        keys_span[SPAN + EDGE : ROWS, :] = jnp.zeros((EDGE, 1024), BF16)

    for d in range(1, PAIRS):
        part_copy(0, pair_before(d), pair_before(d), 0).wait_recv()
        part_copy(0, pair_before(d), pair_before(d), 1).wait_recv()
    part_copy(0, pair, pair, 1 - j).wait_recv()
    for i in range(2):
        summed = parts[0, i]
        for q in range(1, PAIRS):
            summed = summed + parts[q, i]
        turn_c = turn_own[0, 32 * i : 32 * (i + 1), :]
        turn_s = turn_own[1, 32 * i : 32 * (i + 1), :]
        for h in range(2):
            head = summed[:, 128 * h : 128 * (h + 1)]
            turned = head * turn_c + pltpu.roll(head, 64, axis=1) * turn_s
            window[p, h, 32 * i : 32 * (i + 1), :] = turned.astype(BF16)

    def window_copy(chip, source):
        return remote(
            window.at[source],
            window.at[source],
            window_send.at[chip],
            window_recv.at[source],
            core_of(chip),
            z,
        )

    every(1, CHIPS, lambda d: window_copy(lax.rem(p + d, CHIPS), p).start())

    kv_self.wait()

    def kv_wait(source):
        @pl.when(source != p)
        def _():
            remote(
                kv_in.at[j * CHIPS + source],
                kv_in.at[j * CHIPS + source],
                kv_send.at[0],
                kv_recv.at[source],
                core_of(source),
                z,
            ).wait_recv()

    def fwd_copy(n, core):
        part = kv_in.at[pl.ds(core * CHIPS + 4 * n, 4)]
        return remote(part, part, fwd_send.at[n], fwd_recv.at[n], sibling, z)

    for n in range(4):
        every(4 * n, 4 * n + 4, kv_wait)
        fwd_copy(n, j).start()


    @pl.when(p > 0)
    def _():
        edge_copy(True).wait_recv()

    @pl.when(p < CHIPS - 1)
    def _():
        edge_copy(False).wait_recv()

    piece_row = lax.broadcasted_iota(jnp.int32, (PIECE, 256), 0)
    piece_lane = lax.broadcasted_iota(jnp.int32, (PIECE, 256), 1)
    hidden_first = jnp.logical_and(piece_row < EDGE, p == 0)
    last_row = piece_row + (NPIECE - 1) * PIECE
    hidden_last = jnp.logical_or(
        jnp.logical_and(last_row >= SPAN + EDGE, p == CHIPS - 1),
        jnp.logical_and(
            last_row < SPAN + EDGE,
            p * SPAN + last_row - EDGE
            > (2 * CHIPS * POSITIONS - WIN) + jnp.bitwise_and(piece_lane, WIN - 1),
        ),
    )

    def stat_copy(chip, source):
        return remote(
            stat, stat_in.at[source], stat_send.at[chip], stat_recv.at[source], core_of(chip), z
        )

    stat_row = lax.broadcasted_iota(jnp.int32, (CHIPS, 128), 0)

    def window_go(k, carry):
        tops, sums = carry
        for n in range(2):
            source = 2 * k + n

            @pl.when(source != p)
            def _():
                window_copy(0, source).wait_recv()

        rows = window[pl.ds(2 * k, 2)].reshape(256, 128)
        cols = pl.ds(pl.multiple_of(k * 128, 128), 128)
        top = jnp.full((8, 256), LOW, F32)
        for i in range(NPIECE):
            s = dot_nt(keys_span[PIECE * i : PIECE * (i + 1), cols], rows) * SCALE
            if i == 0:
                s = jnp.where(hidden_first, LOW, s)
            if i == NPIECE - 1:
                s = jnp.where(hidden_last, LOW, s)
            exps[k, PIECE * i : PIECE * (i + 1), :] = s
            top = jnp.maximum(top, jnp.max(s.reshape(PIECE // 8, 8, 256), axis=0))
        top = jnp.max(top, axis=0, keepdims=True)
        summed = jnp.zeros((8, 256), F32)
        for i in range(NPIECE):
            e = jnp.exp(exps[k, PIECE * i : PIECE * (i + 1), :] - top)
            exps[k, PIECE * i : PIECE * (i + 1), :] = e
            if i == 0:
                e = e[EDGE:]
            if i == NPIECE - 1:
                e = e[: PIECE - EDGE]
            summed = summed + jnp.sum(e.reshape(-1, 8, 256), axis=0)
        summed = jnp.sum(summed, axis=0, keepdims=True)
        for n in range(2):
            here = stat_row == 2 * k + n
            tops = jnp.where(here, top[:, 128 * n : 128 * (n + 1)], tops)
            sums = jnp.where(here, summed[:, 128 * n : 128 * (n + 1)], sums)
        return tops, sums

    tops, sums = lax.fori_loop(
        0, KEY_HEADS, window_go, (jnp.zeros((CHIPS, 128), F32), jnp.zeros((CHIPS, 128), F32))
    )
    stat[0] = tops
    stat[1] = sums
    every(1, CHIPS, lambda d: stat_copy(lax.rem(p + d, CHIPS), p).start())
    stat_in[p] = stat[...]

    qt_self.wait()

    def qt_wait(r):
        @pl.when(r != slot)
        def _():
            remote(
                qt_in.at[r], qt_in.at[r], qt_send.at[0], qt_recv.at[r], core_of(8 * half + r), z
            ).wait_recv()

    every(0, 8, qt_wait)
    every(0, 4, lambda n: fwd_copy(n, 1 - j).wait_recv())
    rows_q = qt_in[:, 128:160, :].reshape(256, 128)

    def tail_go(r):
        s = dot_nt(qt_in[r, 128:160, :], qt_in[r, 0:128, :]) * SCALE
        tail_scores[r] = s + qt_in[r, 160:QT_ROWS, :].astype(F32)

    each(0, 8, tail_go)
    top = tail_scores[...].reshape(256, 128)

    def score_go(n, top):
        right = kv_in[pl.ds(4 * n, 4), 0:BLOCK, :].reshape(4 * BLOCK, 128)
        s = dot_nt(rows_q, right) * SCALE
        for i in range(4):
            bias = kv_in[4 * n + i, 2 * BLOCK : KV_ROWS, :].astype(F32)[0:1, :]
            one = s[:, BLOCK * i : BLOCK * (i + 1)] + bias
            dec_scores[n, :, BLOCK * i : BLOCK * (i + 1)] = one
            top = jnp.maximum(top, one)
        return top

    top = lax.fori_loop(0, CHIPS // 2, score_go, top)
    top = jnp.max(top, axis=1, keepdims=True)

    def split(weights):
        high = weights.astype(BF16)
        return high, (weights - high.astype(F32)).astype(BF16)

    tail_weights = jnp.exp(tail_scores[...].reshape(256, 128) - top)
    tail_acc = []
    for r in range(8):
        high, low = split(tail_weights[32 * r : 32 * (r + 1), :])
        right = qt_in[r, 64:QT_ROWS, :]
        tail_acc.append(dot(high, right) + dot(low, right))

    def value_go(n, carry):
        acc, weight_sum = carry
        weights = jnp.exp(dec_scores[n] - top)
        high, low = split(weights)
        right = kv_in[pl.ds(4 * n, 4), BLOCK : 2 * BLOCK, :].reshape(4 * BLOCK, 128)
        for i in range(4):
            weight_sum = weight_sum + weights[:, BLOCK * i : BLOCK * (i + 1)]
        return acc + (dot(high, right) + dot(low, right)), weight_sum

    acc, weight_sum = lax.fori_loop(
        0, CHIPS // 2, value_go, (jnp.concatenate(tail_acc, axis=0), tail_weights)
    )
    result = acc / jnp.sum(weight_sum, axis=1, keepdims=True)
    dec_send[...] = result.astype(BF16).reshape(8, 32, 128)

    def dec_copy(r):
        return remote(
            dec_send.at[r],
            dec_in.at[slot],
            dec_send_sem.at[r],
            dec_recv.at[slot],
            core_of(8 * half + r),
            z,
        )

    def dec_go(r):
        @pl.when(r != slot)
        def _():
            dec_copy(r).start()

    every(0, 8, dec_go)
    dec_self = pltpu.make_async_copy(dec_send.at[slot], dec_in.at[slot], local_sem.at[7])
    dec_self.start()

    every(
        1,
        CHIPS,
        lambda d: stat_copy(
            lax.rem(p + CHIPS - d, CHIPS), lax.rem(p + CHIPS - d, CHIPS)
        ).wait_recv(),
    )
    peak = stat_in[0, 0]
    for o in range(1, CHIPS):
        peak = jnp.maximum(peak, stat_in[o, 0])
    merged = jnp.zeros((CHIPS, 128), F32)
    for o in range(CHIPS):
        merged = merged + stat_in[o, 1] * jnp.exp(stat_in[o, 0] - peak)
    factor = jnp.exp(stat[0] - peak) / merged

    factors = [factor[o : o + 1, :] for o in range(CHIPS)]
    head_lane = lax.broadcasted_iota(jnp.int32, (PIECE, 128), 1)
    for i in range(NPIECE):
        rows = slice(PIECE * i, PIECE * (i + 1))
        votes = jnp.zeros((PIECE, 128), F32)
        for k in range(KEY_HEADS):
            weighted = (
                exps[k, rows, 0:128] * factors[2 * k] + exps[k, rows, 128:256] * factors[2 * k + 1]
            )
            votes = jnp.where(head_lane == k, jnp.sum(weighted, axis=1, keepdims=True), votes)
        columns[rows, :] = votes
    columns[ROWS:, :] = jnp.zeros((columns.shape[0] - ROWS, 128), F32)
    lanes = columns.shape[0]
    across = jnp.transpose(columns[...])[0:KEY_HEADS, :]
    near = POOL // 2
    window_sum = jnp.zeros((KEY_HEADS, lanes), F32)
    for shift in range(EDGE - near, EDGE + near + 1):
        window_sum = window_sum + pltpu.roll(across, lanes - shift, axis=1)
    for n in range(2):
        pooled[n] = window_sum[:, POSITIONS * n : POSITIONS * (n + 1)]
    share_votes = remote(pooled.at[1 - j], pooled_in, pair_send.at[4], pair_recv.at[4], sibling, z)
    share_votes.start()

    dec_self.wait()

    def dec_wait(k):
        @pl.when(k != slot)
        def _():
            remote(
                dec_send.at[k], dec_in.at[k], dec_send_sem.at[0], dec_recv.at[k], core_of(8 * half + k), z
            ).wait_recv()

    every(0, 8, dec_wait)
    decode_out[...] = dec_in[...]

    share_votes.wait_recv()
    votes_out[...] = (pooled[j] + pooled_in[...]) * (
        2 * CHIPS * POSITIONS / (WIN * 8) / POOL
    )

    share_votes.wait_send()
    share_w.wait_send()
    share_k.wait_send()

    @pl.when(p < CHIPS - 1)
    def _():
        edge_copy(True).wait_send()

    @pl.when(p > 0)
    def _():
        edge_copy(False).wait_send()

    for d in range(1, PAIRS):
        q = lax.rem(pair + d, PAIRS)
        piece_copy(q, pair).wait_send()
        part_copy(0, q, pair, j).wait_send()
        part_copy(1, q, pair, j).wait_send()
    part_copy(1 - j, pair, pair, j).wait_send()
    for n in range(2):
        weight_copy(n).wait_send()
        weight_on(n).wait_send()

    def sent_chip(d):
        chip = lax.rem(p + d, CHIPS)
        gather_copy(chip, p).wait_send()
        window_copy(chip, p).wait_send()
        stat_copy(chip, p).wait_send()
        kv_copy(chip % 8, chip // 8).wait_send()

    each(1, CHIPS, sent_chip)
    each(0, 4, lambda n: fwd_copy(n, j).wait_send())

    def sent_slot(k):
        @pl.when(k != slot)
        def _():
            qt_copy(k).wait_send()
            dec_copy(k).wait_send()

    each(0, 8, sent_slot)


def on_device(
    window_states,
    query_weight,
    cache_keys,
    cache_values,
    kept_blocks,
    retained_block_count,
    decode_queries,
    tail_keys,
    tail_values,
    row_lengths,
):
    queries = (
        decode_queries.reshape(STEPS, KEY_HEADS, 8, HEAD_DIMENSION)
        .transpose(1, 0, 2, 3)
        .reshape(KEY_HEADS, 32, HEAD_DIMENSION)
    )
    hbm = pl.BlockSpec(memory_space=pl.ANY)
    vmem = pl.BlockSpec(memory_space=pltpu.VMEM)
    dma = pltpu.SemaphoreType.DMA
    votes, decoded = pl.pallas_call(
        body,
        out_shape=(
            jax.ShapeDtypeStruct((KEY_HEADS, POSITIONS), F32),
            jax.ShapeDtypeStruct((KEY_HEADS, 32, HEAD_DIMENSION), BF16),
        ),
        in_specs=[hbm] * 11,
        out_specs=(vmem, vmem),
        scratch_shapes=[
            pltpu.VMEM((2, 2, 1024, 256), BF16),
            pltpu.VMEM((POSITIONS, 1024), BF16),
            pltpu.VMEM((POSITIONS, 1024), BF16),
            pltpu.VMEM((ROWS, 1024), BF16),
            pltpu.VMEM((CHIPS, PAIRS, 16, 256), BF16),
            pltpu.VMEM((2, PAIRS, 32, 256), F32),
            pltpu.VMEM((PAIRS, 2, 32, 256), F32),
            pltpu.VMEM((CHIPS, 2, WIN, 128), BF16),
            pltpu.VMEM((KEY_HEADS, ROWS, 256), F32),
            pltpu.VMEM((2, CHIPS, 128), F32),
            pltpu.VMEM((CHIPS, 2, CHIPS, 128), F32),
            pltpu.VMEM((ROWS + 96, 128), F32),
            pltpu.VMEM((2, KEY_HEADS, POSITIONS), F32),
            pltpu.VMEM((KEY_HEADS, POSITIONS), F32),
            pltpu.VMEM((KEY_HEADS, KV_ROWS, 128), BF16),
            pltpu.VMEM((2 * CHIPS, KV_ROWS, 128), BF16),
            pltpu.VMEM((KEY_HEADS, QT_ROWS, 128), BF16),
            pltpu.VMEM((8, QT_ROWS, 128), BF16),
            pltpu.VMEM((CHIPS // 2, 256, 4 * BLOCK), F32),
            pltpu.VMEM((8, 32, 128), F32),
            pltpu.VMEM((8, 32, 128), BF16),
            pltpu.VMEM((8, 32, 128), BF16),
            pltpu.VMEM((1, 8), jnp.int32),
            pltpu.VMEM((1, 8), jnp.int32),
            pltpu.VMEM((1, 1), jnp.int32),
            pltpu.VMEM((2, WIN, 128), F32),
            pltpu.VMEM((KEY_HEADS, 32, 128), BF16),
            dma((40,)),
            dma((PAIRS,)),
            dma((PAIRS,)),
            dma((CHIPS,)),
            dma((CHIPS,)),
            dma((5,)),
            dma((5,)),
            dma((2, PAIRS)),
            dma((PAIRS, 2)),
            dma((CHIPS,)),
            dma((CHIPS,)),
            dma((CHIPS,)),
            dma((CHIPS,)),
            dma((4,)),
            dma((4,)),
            dma((CHIPS,)),
            dma((CHIPS,)),
            dma((4,)),
            dma((4,)),
            dma((8,)),
            dma((8,)),
            dma((8,)),
            dma((8,)),
        ],
        compiler_params=pltpu.CompilerParams(
            collective_id=0, has_side_effects=True, vmem_limit_bytes=60 * 1024 * 1024
        ),
        cost_estimate=pl.CostEstimate(
            flops=1_400_000_000, bytes_accessed=6_000_000, transcendentals=3_500_000
        ),
    )(
        window_states,
        query_weight,
        cache_keys,
        cache_values,
        kept_blocks.reshape(1, KEY_HEADS),
        retained_block_count.reshape(1, KEY_HEADS),
        queries,
        tail_keys,
        tail_values,
        row_lengths,
        jnp.asarray(rotary_table()),
    )
    decoded = (
        decoded.reshape(KEY_HEADS, STEPS, 8, HEAD_DIMENSION)
        .transpose(1, 0, 2, 3)
        .reshape(1, STEPS, 1, KEY_HEADS * 8 * HEAD_DIMENSION)
    )
    return votes[None], decoded


def solution(mesh):
    placed = (
        P("grp", None, None),
        P("grp", "ctx"),
        P("grp", "ctx", None),
        P("grp", "ctx", None),
        P("grp", None, "ctx"),
        P("grp", None, "ctx"),
        P("grp", None, "ctx", None),
        P("grp", "ctx", None, None),
        P("grp", "ctx", None, None),
        P("grp", "ctx"),
    )
    return jax.shard_map(
        on_device,
        mesh=mesh,
        in_specs=placed,
        out_specs=(P("grp", None, "ctx"), P("grp", None, "ctx", None)),
        check_vma=False,
    )
```

time: 91.4 us -> 71.1 us (0.78)
  Pallas kernels: 78.8 us -> 65.6 us
  local copies, waits for them, and re-layouts: 10.7 us -> 3.65 us
    pallas_call x1, Pallas kernels: 78.8 us -> 65.6 us  [on_device(): pl.pallas_call(body, out_shape=(jax.ShapeDtypeStruct((KEY_HEADS, POSITION...]
    unnamed x19 -> x3, local copies, waits for them, and re-layouts: 9.2 us -> 0.66 us
where the time goes in v2:
time: 71.1 us; the launch traced here: 70.6 us
  Pallas kernels  65.6 us (92%)
  local copies, waits for them, and re-layouts  3.65 us (5%)
  between operations  1.3 us (2%)
    pallas_call x1, Pallas kernels, on_device(): pl.pallas_call(body, out_shape=(jax.ShapeDtypeStruct((KEY_HEADS, POSITION...  65.6 us
    reshape x1, local copies, waits for them, and re-layouts, on_device(): queries = decode_queries.reshape(STEPS, KEY_HEADS, 8, HEAD_DIMENSION).tra...  1.48 us

profile of v2, /device:TPU:1, one launch (start us, length us, event | category | flops | bytes accessed | tf_op | source)
XLA Modules:
  0.0 70.6 jit_solution(14076561579864251002)
XLA Ops:
  1.3 1.5 %copy_bitcast_fusion.1.queries = bf16[8,32,128]{2,1,0:T(8,128)(2,1)} fusion(bf16[1,4,64,128]{3,1,2,0:T(4,128)(2,1)} %bitcast.19), kind=kLoop, calls=%fused_computation.1 | loop fusion | bytes 131072 | tf_op jit(solution)/shard_map/reshape | solution.py:739
  2.8 65.6 %shard_map.122 = (f32[8,512]{1,0:T(8,128)}, bf16[8,32,128]{2,1,0:T(8,128)(2,1)}) custom-call(bf16[1,64,8192]{2,1,0:T(8,128)(2,1)} %states.1, bf16[1024,256]{1,0:T(8,128)(2,1)} %weight.1, bf16[1,512,1024]{2,1,0:T(8,128)(2,1)} %keys.1, bf16[1,512,1024]{2,1,0:T(8,128)(2,1)} %values.1, s32[1,8]{1,0:T(1,128)} %bitcast.22, s32[1,8]{1,0:T(1,128)} %bitcast.23, ...), custom_call_target="tpu_custom_call" | custom-call | flops 1400000000 | bytes 6000000 | tf_op jit(solution)/shard_map/pallas_call | solution.py:744
  68.4 0.9 %copy.14 = bf16[4,8,8,128]{3,2,1,0:T(8,128)(2,1)S(1)} copy(bf16[4,8,8,128]{3,2,0,1:T(8,128)(2,1)} %bitcast.20) | data formatting | bytes 131072 | tf_op jit(solution)/shard_map/transpose | solution.py:825
  69.3 0.0 copy-start
  69.3 0.7 reshape.27
  69.9 0.1 copy-done
  70.0 0.6 copy.21
Async XLA Ops:
  69.3 0.7 %copy-start = (f32[8,512]{1,0:T(8,128)S(1)}, f32[8,512]{1,0:T(8,128)}, u32[]{:S(2)}) copy-start(f32[8,512]{1,0:T(8,128)} %get-tuple-element.4) | copy-start | bytes 49156

commit v3 on v2

--- a/solution.py
+++ b/solution.py
@@ -102,6 +102,7 @@
     lengths_own,
     turn_own,
     queries_own,
+    rows_wide,
     local_sem,
     piece_send,
     piece_recv,
@@ -241,13 +242,15 @@
             )
         live = jnp.broadcast_to(counts_own[:, k : k + 1], (16, 128)) > 0
         kv_out[k, 2 * BLOCK : KV_ROWS, :] = jnp.where(live, 0.0, LOW).astype(BF16)
-    step_row = lax.broadcasted_iota(jnp.int32, (32, 128), 0) // 8
+    step_row = lax.broadcasted_iota(jnp.int32, (32, 128), 0) % STEPS
     lane = lax.broadcasted_iota(jnp.int32, (32, 128), 1)
     tail_bias = jnp.where(
         lane < jnp.broadcast_to(lengths_own[...], (32, 128)) + step_row, 0.0, LOW
     ).astype(BF16)
     for k in range(KEY_HEADS):
-        qt_out[k, 128:160, :] = queries_own[k]
+        for h in range(8):
+            rows_wide[32 * k + 4 * h : 32 * k + 4 * (h + 1), :] = queries_own[8 * k + h].astype(F32)
+        qt_out[k, 128:160, :] = rows_wide[32 * k : 32 * (k + 1), :].astype(BF16)
         qt_out[k, 160:QT_ROWS, :] = tail_bias
 
     pl.semaphore_wait(barrier, CHIPS - 1 + 1 + 2 * (PAIRS - 1) + 1)
@@ -339,15 +342,6 @@
     qt_self = pltpu.make_async_copy(qt_out.at[slot], qt_in.at[slot], local_sem.at[6])
     qt_self.start()
 
-    every(1, CHIPS, kv_go)
-
-    def qt_go(k):
-        @pl.when(k != slot)
-        def _():
-            qt_copy(k).start()
-
-    every(0, KEY_HEADS, qt_go)
-
     load_w.wait()
     share_w.wait_recv()
     every(
@@ -357,6 +351,15 @@
             lax.rem(p + CHIPS - d, CHIPS), lax.rem(p + CHIPS - d, CHIPS)
         ).wait_recv(),
     )
+
+    every(1, CHIPS, kv_go)
+
+    def qt_go(k):
+        @pl.when(k != slot)
+        def _():
+            qt_copy(k).start()
+
+    every(0, KEY_HEADS, qt_go)
 
     def left_of(m):
         return jnp.concatenate(
@@ -673,7 +676,9 @@
             ).wait_recv()
 
     every(0, 8, dec_wait)
-    decode_out[...] = dec_in[...]
+    rows_wide[...] = dec_in[...].astype(F32).reshape(256, 128)
+    for h in range(64):
+        decode_out[h] = rows_wide[4 * h : 4 * (h + 1), :].astype(BF16)
 
     share_votes.wait_recv()
     votes_out[...] = (pooled[j] + pooled_in[...]) * (
@@ -733,11 +738,7 @@
     tail_values,
     row_lengths,
 ):
-    queries = (
-        decode_queries.reshape(STEPS, KEY_HEADS, 8, HEAD_DIMENSION)
-        .transpose(1, 0, 2, 3)
-        .reshape(KEY_HEADS, 32, HEAD_DIMENSION)
-    )
+    queries = decode_queries.reshape(STEPS, 64, HEAD_DIMENSION).transpose(1, 0, 2)
     hbm = pl.BlockSpec(memory_space=pl.ANY)
     vmem = pl.BlockSpec(memory_space=pltpu.VMEM)
     dma = pltpu.SemaphoreType.DMA
@@ -745,7 +746,7 @@
         body,
         out_shape=(
             jax.ShapeDtypeStruct((KEY_HEADS, POSITIONS), F32),
-            jax.ShapeDtypeStruct((KEY_HEADS, 32, HEAD_DIMENSION), BF16),
+            jax.ShapeDtypeStruct((64, STEPS, HEAD_DIMENSION), BF16),
         ),
         in_specs=[hbm] * 11,
         out_specs=(vmem, vmem),
@@ -776,7 +777,8 @@
             pltpu.VMEM((1, 8), jnp.int32),
             pltpu.VMEM((1, 1), jnp.int32),
             pltpu.VMEM((2, WIN, 128), F32),
-            pltpu.VMEM((KEY_HEADS, 32, 128), BF16),
+            pltpu.VMEM((64, STEPS, 128), BF16),
+            pltpu.VMEM((256, 128), F32),
             dma((40,)),
             dma((PAIRS,)),
             dma((PAIRS,)),
@@ -820,11 +822,7 @@
         row_lengths,
         jnp.asarray(rotary_table()),
     )
-    decoded = (
-        decoded.reshape(KEY_HEADS, STEPS, 8, HEAD_DIMENSION)
-        .transpose(1, 0, 2, 3)
-        .reshape(1, STEPS, 1, KEY_HEADS * 8 * HEAD_DIMENSION)
-    )
+    decoded = decoded.transpose(1, 0, 2).reshape(1, STEPS, 1, 64 * HEAD_DIMENSION)
     return votes[None], decoded
 
 

time: 71.1 us -> 68.6 us (0.965)
  Pallas kernels: 65.6 us -> 64.3 us
  local copies, waits for them, and re-layouts: 3.65 us -> 2.82 us
    unnamed x3 -> x2, local copies, waits for them, and re-layouts: 0.66 us -> 2.82 us
    reshape x2 -> x0, local copies, waits for them, and re-layouts: 2.13 us -> none  [the longest x1 1.48 us: on_device(): queries = decode_queries.reshape(STEPS, KEY_HEADS, 8, HEAD_DIMENSION).tra...]
    pallas_call x1, Pallas kernels: 65.6 us -> 64.3 us  [on_device(): pl.pallas_call(body, out_shape=(jax.ShapeDtypeStruct((KEY_HEADS, POSITION...]
    transpose x1 -> x0, local copies, waits for them, and re-layouts: 0.85 us -> none  [on_device(): decoded = decoded.reshape(KEY_HEADS, STEPS, 8, HEAD_DIMENSION).transpose(...]
where the time goes in v3:
time: 68.6 us; the launch traced here: 68.4 us
  Pallas kernels  64.3 us (94%)
  local copies, waits for them, and re-layouts  2.82 us (4%)
  between operations  1.29 us (2%)
    pallas_call x1, Pallas kernels, on_device(): pl.pallas_call(body, out_shape=(jax.ShapeDtypeStruct((KEY_HEADS, POSITION...  64.3 us
    unnamed x2, local copies, waits for them, and re-layouts  2.82 us

profile of v3, /device:TPU:1, one launch (start us, length us, event | category | flops | bytes accessed | tf_op | source)
XLA Modules:
  0.0 68.4 jit_solution(15522623857992313130)
XLA Ops:
  1.3 64.3 %shard_map.122 = (f32[8,512]{1,0:T(8,128)}, bf16[64,4,128]{2,1,0:T(4,128)(2,1)}) custom-call(bf16[1,64,8192]{2,1,0:T(8,128)(2,1)} %states.1, bf16[1024,256]{1,0:T(8,128)(2,1)} %weight.1, bf16[1,512,1024]{2,1,0:T(8,128)(2,1)} %keys.1, bf16[1,512,1024]{2,1,0:T(8,128)(2,1)} %values.1, s32[1,8]{1,0:T(1,128)} %bitcast.12, s32[1,8]{1,0:T(1,128)} %bitcast.13, ...), custom_call_target="tpu_custom_call" | custom-call | flops 1400000000 | bytes 6000000 | tf_op jit(solution)/shard_map/pallas_call | solution.py:745
  65.6 1.3 %copy.16 = f32[1,8,512]{2,1,0:T(8,128)} copy(f32[1,8,512]{2,1,0:T(8,128)} %bitcast.10) | data formatting | bytes 32768
  66.9 1.5 %copy.17 = bf16[1,4,1,8192]{3,1,2,0:T(4,128)(2,1)} copy(bf16[1,4,1,8192]{3,1,2,0:T(4,128)(2,1)} %bitcast.9) | data formatting | bytes 131072

commit v4 on v3

--- a/solution.py
+++ b/solution.py
@@ -477,6 +477,37 @@
         fwd_copy(n, j).start()
 
 
+    qt_self.wait()
+
+    def qt_wait(r):
+        @pl.when(r != slot)
+        def _():
+            remote(
+                qt_in.at[r], qt_in.at[r], qt_send.at[0], qt_recv.at[r], core_of(8 * half + r), z
+            ).wait_recv()
+
+    every(0, 8, qt_wait)
+    rows_q = qt_in[:, 128:160, :].reshape(256, 128)
+
+    def tail_go(r):
+        s = dot_nt(qt_in[r, 128:160, :], qt_in[r, 0:128, :]) * SCALE
+        tail_scores[r] = s + qt_in[r, 160:QT_ROWS, :].astype(F32)
+
+    each(0, 8, tail_go)
+    top = tail_scores[...].reshape(256, 128)
+
+    def score_go(n, top):
+        right = kv_in[pl.ds(4 * n, 4), 0:BLOCK, :].reshape(4 * BLOCK, 128)
+        s = dot_nt(rows_q, right) * SCALE
+        for i in range(4):
+            bias = kv_in[4 * n + i, 2 * BLOCK : KV_ROWS, :].astype(F32)[0:1, :]
+            one = s[:, BLOCK * i : BLOCK * (i + 1)] + bias
+            dec_scores[n, :, BLOCK * i : BLOCK * (i + 1)] = one
+            top = jnp.maximum(top, one)
+        return top
+
+    top_near = lax.fori_loop(0, 4, lambda n, t: score_go(4 * j + n, t), top)
+
     @pl.when(p > 0)
     def _():
         edge_copy(True).wait_recv()
@@ -550,37 +581,8 @@
     every(1, CHIPS, lambda d: stat_copy(lax.rem(p + d, CHIPS), p).start())
     stat_in[p] = stat[...]
 
-    qt_self.wait()
-
-    def qt_wait(r):
-        @pl.when(r != slot)
-        def _():
-            remote(
-                qt_in.at[r], qt_in.at[r], qt_send.at[0], qt_recv.at[r], core_of(8 * half + r), z
-            ).wait_recv()
-
-    every(0, 8, qt_wait)
     every(0, 4, lambda n: fwd_copy(n, 1 - j).wait_recv())
-    rows_q = qt_in[:, 128:160, :].reshape(256, 128)
-
-    def tail_go(r):
-        s = dot_nt(qt_in[r, 128:160, :], qt_in[r, 0:128, :]) * SCALE
-        tail_scores[r] = s + qt_in[r, 160:QT_ROWS, :].astype(F32)
-
-    each(0, 8, tail_go)
-    top = tail_scores[...].reshape(256, 128)
-
-    def score_go(n, top):
-        right = kv_in[pl.ds(4 * n, 4), 0:BLOCK, :].reshape(4 * BLOCK, 128)
-        s = dot_nt(rows_q, right) * SCALE
-        for i in range(4):
-            bias = kv_in[4 * n + i, 2 * BLOCK : KV_ROWS, :].astype(F32)[0:1, :]
-            one = s[:, BLOCK * i : BLOCK * (i + 1)] + bias
-            dec_scores[n, :, BLOCK * i : BLOCK * (i + 1)] = one
-            top = jnp.maximum(top, one)
-        return top
-
-    top = lax.fori_loop(0, CHIPS // 2, score_go, top)
+    top = lax.fori_loop(0, 4, lambda n, t: score_go(4 * (1 - j) + n, t), top_near)
     top = jnp.max(top, axis=1, keepdims=True)
 
     def split(weights):

time: 68.6 us -> 70.1 us (1.022)
  Pallas kernels: 64.3 us -> 65.8 us
    pallas_call x1, Pallas kernels: 64.3 us -> 65.8 us  [on_device(): pl.pallas_call(body, out_shape=(jax.ShapeDtypeStruct((KEY_HEADS, POSITION...]
where the time goes in v4:
time: 70.1 us; the launch traced here: 69.9 us
  Pallas kernels  65.8 us (94%)
  local copies, waits for them, and re-layouts  2.82 us (4%)
  between operations  1.29 us (2%)
    pallas_call x1, Pallas kernels, on_device(): pl.pallas_call(body, out_shape=(jax.ShapeDtypeStruct((KEY_HEADS, POSITION...  65.8 us
    unnamed x2, local copies, waits for them, and re-layouts  2.82 us

profile of v4, /device:TPU:1, one launch (start us, length us, event | category | flops | bytes accessed | tf_op | source)
XLA Modules:
  0.0 69.9 jit_solution(11465744877308930457)
XLA Ops:
  1.3 65.8 %shard_map.122 = (f32[8,512]{1,0:T(8,128)}, bf16[64,4,128]{2,1,0:T(4,128)(2,1)}) custom-call(bf16[1,64,8192]{2,1,0:T(8,128)(2,1)} %states.1, bf16[1024,256]{1,0:T(8,128)(2,1)} %weight.1, bf16[1,512,1024]{2,1,0:T(8,128)(2,1)} %keys.1, bf16[1,512,1024]{2,1,0:T(8,128)(2,1)} %values.1, s32[1,8]{1,0:T(1,128)} %bitcast.12, s32[1,8]{1,0:T(1,128)} %bitcast.13, ...), custom_call_target="tpu_custom_call" | custom-call | flops 1400000000 | bytes 6000000 | tf_op jit(solution)/shard_map/pallas_call | solution.py:747
  67.1 1.3 %copy.16 = f32[1,8,512]{2,1,0:T(8,128)} copy(f32[1,8,512]{2,1,0:T(8,128)} %bitcast.10) | data formatting | bytes 32768
  68.4 1.5 %copy.17 = bf16[1,4,1,8192]{3,1,2,0:T(4,128)(2,1)} copy(bf16[1,4,1,8192]{3,1,2,0:T(4,128)(2,1)} %bitcast.9) | data formatting | bytes 131072
